TPU v7x, 32 devices: a whole 2x2x4 slice. The times are simulated.
32 devices in a mesh: seg: 4 (over z_hi, core), shard: 4 (over y, x), tok: 2 (over z_lo).
Axes of the slice: x: 2, y: 2, z: 4 (z_hi: 2, z_lo: 2; z = z_hi * 2 + z_lo), core: 2. Of those that a mesh axis runs over, the one named last changes fastest.
Arguments:
- activations: bfloat16 [768, 2560], P('tok', 'shard'), may hold values from -6 to 6
- gate_weight: bfloat16 [2560, 10240], P('shard', 'seg'), may hold values from -0.125 to 0.125
- up_weight: bfloat16 [2560, 10240], P('shard', 'seg'), may hold values from -0.125 to 0.125
- down_weight: bfloat16 [10240, 2560], P('seg', 'shard'), may hold values from -0.0625 to 0.0625
- encoder_weight: bfloat16 [2560, 8192], P(None, ('seg', 'shard')), may hold values from -0.125 to 0.125
- encoder_bias: float32 [8192], P(('seg', 'shard')), may hold values from -0.6 to 0.2
- decoder_weight: bfloat16 [8192, 2560], P(('seg', 'shard')), may hold values from -0.125 to 0.125
- decoder_bias: float32 [2560], replicated, may hold values from -1.5 to 1.5
- segment_sizes: int32 [4], replicated, may hold values from 1024 to 2048, as said below
Outputs:
- grad_encoder: float32 [2560, 8192], P('tok', ('seg', 'shard'))
- grad_decoder: float32 [8192, 2560], P(('seg', 'shard'), 'tok')
- prefix_mse: float32 [4], P('seg')
Inputs may be any that keep to these rules, and one draw needn't show every extreme that they name: `segment_sizes`: at least one segment has all 2048 latents live.
All inputs are finite; a program needn't handle non-finite values.
Results may differ from a plain program's by a relative error of at most 0.0078.
Values may be sent and summed in bfloat16 or wider, within the bound.
A program may use at most 64 MiB of HBM per device.

v0:
```python
import math

import jax
import jax.numpy as jnp
from jax import lax
from jax.sharding import PartitionSpec as P


def carried_in(value, axis, join, neutral, backward):
    count, mine = (lax.axis_size(axis), lax.axis_index(axis))
    pieces = lax.all_gather(value, axis)
    if backward:
        pieces = pieces[::-1]
        mine = count - 1 - mine
    subtotal = jnp.full_like(value, 0) + jnp.asarray(neutral, value.dtype)

    def hop(position, subtotal):
        longer = join(subtotal, pieces[position])
        return jnp.where(position < mine, longer, subtotal)

    return lax.fori_loop(0, count - 1, hop, subtotal)


def local(
    activations,
    gate_weight,
    up_weight,
    down_weight,
    encoder_weight,
    encoder_bias,
    decoder_weight,
    decoder_bias,
    segment_sizes,
):
    shard_index = lax.axis_index("shard")
    segment_index = lax.axis_index("seg")
    group_index = lax.axis_index("tok")
    tok_rows = activations.shape[0]
    width_slice = activations.shape[1]
    gate_part = jnp.dot(activations, gate_weight, preferred_element_type=jnp.float32)
    up_part = jnp.dot(activations, up_weight, preferred_element_type=jnp.float32)
    gate_total, up_total = lax.psum((gate_part, up_part), "shard")
    hidden = (jax.nn.gelu(gate_total, approximate=True) * up_total).astype(jnp.bfloat16)
    down_part = jnp.dot(hidden, down_weight, preferred_element_type=jnp.float32)
    mlp_slice = lax.psum(down_part, "seg").astype(jnp.bfloat16)
    mlp_full = lax.all_gather(mlp_slice, "shard", axis=1, tiled=True)
    width = mlp_full.shape[1]
    groups = lax.axis_size("tok")
    tokens_all = tok_rows * groups
    half_width = width // groups
    mlp_float = mlp_full.astype(jnp.float32)
    centered = (mlp_float - decoder_bias).astype(jnp.bfloat16)
    lat_count = encoder_weight.shape[1]
    segment_total = segment_sizes.shape[0]
    size_here = jnp.sum(jnp.where(jnp.arange(segment_total) == segment_index, segment_sizes, 0))
    latent_index = shard_index * lat_count + jnp.arange(lat_count)
    live_mask = latent_index < size_here
    pre_act = jnp.dot(centered, encoder_weight, preferred_element_type=jnp.float32) + encoder_bias
    latent_codes = jnp.where(live_mask, jax.nn.softplus(10.0 * pre_act) / 10.0, 0.0).astype(
        jnp.bfloat16
    )
    slope = jnp.where(live_mask, jax.nn.sigmoid(10.0 * pre_act), 0.0)
    codes_all = lax.all_gather(latent_codes, "tok", axis=0, tiled=True)
    centered_all = lax.all_to_all(centered, "tok", split_axis=1, concat_axis=0, tiled=True)
    columns = decoder_weight
    my_part = lax.psum_scatter(
        lax.dot_general(
            columns, latent_codes, (((0,), (1,)), ((), ())), preferred_element_type=jnp.float32
        ),
        "shard",
        scatter_dimension=0,
        tiled=True,
    )
    column_start = shard_index * width_slice
    target = lax.dynamic_slice_in_dim(mlp_float, column_start, width_slice, 1).T
    bias_slice = lax.dynamic_slice_in_dim(decoder_bias, column_start, width_slice, 0)[:, None]
    blank = jnp.zeros_like(my_part)
    earlier = carried_in(my_part, "seg", jnp.add, blank, False)
    errors = bias_slice + (earlier + my_part) - target
    total_square = lax.psum(jnp.sum(errors * errors), ("shard", "tok"))
    prefix_mse = (total_square / (tokens_all * width)).reshape(1)
    later = carried_in(errors, "seg", jnp.add, blank, True)
    back = ((later + errors) * (1.0 / math.sqrt(tokens_all))).astype(jnp.bfloat16)
    back_all = lax.all_gather(back, "tok", axis=1, tiled=True)
    piece = lax.all_gather(back_all, "shard", axis=0, tiled=True)
    columns = decoder_weight
    own_piece = lax.dynamic_slice_in_dim(piece, group_index * tok_rows, tok_rows, 1)
    code_acc = lax.dot_general(
        own_piece, columns, (((0,), (1,)), ((), ())), preferred_element_type=jnp.float32
    )
    grad_piece = lax.dot_general(
        codes_all, piece, (((0,), (1,)), ((), ())), preferred_element_type=jnp.float32
    )
    code_grad = (code_acc * slope).astype(jnp.bfloat16)
    code_grad_all = lax.all_gather(code_grad, "tok", axis=0, tiled=True)
    grad_encoder = lax.dot_general(
        centered_all, code_grad_all, (((0,), (0,)), ((), ())), preferred_element_type=jnp.float32
    )
    grad_decoder = lax.dynamic_slice_in_dim(grad_piece, group_index * half_width, half_width, 1)
    return (grad_encoder, grad_decoder, prefix_mse)


def solution(mesh):
    in_specs = (
        P("tok", "shard"),
        P("shard", "seg"),
        P("shard", "seg"),
        P("seg", "shard"),
        P(None, ("seg", "shard")),
        P(("seg", "shard")),
        P(("seg", "shard"), None),
        P(),
        P(),
    )
    out_specs = (P("tok", ("seg", "shard")), P(("seg", "shard"), "tok"), P("seg"))
    return jax.shard_map(local, mesh=mesh, in_specs=in_specs, out_specs=out_specs, check_vma=False)
```

profile of v0, /device:TPU:10, one launch (start us, length us, event | category | flops | bytes accessed | tf_op | source)
XLA Modules:
  0.0 562.2 jit_solution(16881924125009914527)
XLA Ops:
  7.2 1.9 copy-done
  9.1 4.8 fusion.29
  13.9 3.6 fusion.30
  17.5 0.0 all-gather.7.cloned.1.call-start
  17.6 166.0 %all-reduce.4.cloned.1.call-done = (f32[384,2560]{1,0:T(8,128)}, f32[384,2560]{1,0:T(8,128)}) async-done(((f32[384,2560]{1,0:T(8,128)}, f32[384,2560]{1,0:T(8,128)}), (f32[384,2560]{1,0:T(8,128)}, f32[384,2560]{1,0:T(8,128)})) %all-reduce.4.cloned.1.call-update) | async-done | bytes 7864336 | tf_op jit(solution)/shard_map/psum | solution.py:42
  183.6 6.8 %fusion.11 = f32[384,640]{1,0:T(8,128)S(1)} fusion(bf16[2560,640]{1,0:T(8,128)(2,1)} %param.16, f32[384,2560]{1,0:T(8,128)} %get-tuple-element.217, f32[384,2560]{1,0:T(8,128)} %get-tuple-element.218), kind=kOutput, calls=%fused_computation.18 | convolution fusion | flops 1268121600 | bytes 12124160 | tf_op jit(solution)/shard_map/dot_general | solution.py:44
  190.3 38.9 %all-reduce.5 = bf16[384,640]{1,0:T(8,128)(2,1)} all-reduce(f32[384,640]{1,0:T(8,128)S(1)} %fusion.11), channel_id=1, replica_groups=mesh['seg'=4,'shard'=4,'tok'=2] {'seg'}, use_global_device_ids=true, to_apply=%region_2.0 | all-reduce | flops 245760 | bytes 1474560 | tf_op jit(solution)/shard_map/psum | solution.py:45
  229.3 0.0 reduce-scatter.2.cloned.1.call-start
  229.4 0.6 fusion.24
  230.0 0.7 add_compare_fusion
  230.7 34.0 %all-gather.7.cloned.1.call-done = bf16[384,2560]{1,0:T(8,128)(2,1)} async-done(((bf16[384,640]{1,0:T(8,128)(2,1)}), bf16[384,2560]{1,0:T(8,128)(2,1)}) %all-gather.7.cloned.1.call-update) | async-done | bytes 1966096 | tf_op jit(solution)/shard_map/all_gather | solution.py:46
  264.6 2.0 subtract_convert_fusion
  266.7 0.3 copy-done.13
  267.0 2.6 fusion.22
  269.6 0.8 copy-done.10
  270.3 3.1 convolution_bitcast_fusion
  273.4 0.0 all-gather.11.cloned.1.call-start
  273.5 50.6 %reduce-scatter.2.cloned.1.call-done = f32[640,384]{0,1:T(8,128)} async-done(((f32[2560,384]{0,1:T(8,128)}), f32[640,384]{0,1:T(8,128)}) %reduce-scatter.2.cloned.1.call-update) | async-done | bytes 983056 | tf_op jit(solution)/shard_map/reduce_scatter | solution.py:66
  324.1 0.1 dynamic_slice.26
  324.2 2.4 convert_element_type.23
  326.5 49.7 %all-gather.11.cloned.1.call-done = f32[2560,384]{0,1:T(8,128)} async-done(((f32[640,384]{0,1:T(8,128)}), f32[2560,384]{0,1:T(8,128)}) %all-gather.11.cloned.1.call-update) | async-done | bytes 3932176 | tf_op jit(solution)/shard_map/all_gather | solution.py:11
  376.2 5.6 copy.21
  381.8 4.5 while.28
  381.8 1.5 add_select_fusion.4
  383.4 1.4 add_select_fusion.4
  384.8 1.4 add_select_fusion.4
  386.3 0.3 copy.18
  386.6 3.0 multiply_reduce_fusion
  389.7 0.0 all-gather.9.cloned.1.call-start
  389.7 54.1 %all-gather.13.cloned.1.call-done = f32[2560,384]{0,1:T(8,128)} async-done(((f32[640,384]{0,1:T(8,128)}), f32[2560,384]{0,1:T(8,128)}) %all-gather.13.cloned.1.call-update) | async-done | bytes 3932176 | tf_op jit(solution)/shard_map/all_gather | solution.py:11
  443.8 5.5 copy.22
  449.4 4.2 rev.3
  453.6 4.5 while.29
  453.6 1.5 add_select_fusion.5
  455.1 1.4 add_select_fusion.5
  456.6 1.4 add_select_fusion.5
  458.1 0.3 copy.20
  458.4 0.1 multiply_convert_fusion
  458.5 17.3 %all_gather.32 = bf16[640,768]{0,1:T(8,128)(2,1)} all-gather(bf16[640,384]{0,1:T(8,128)(2,1)S(1)} %multiply_convert_fusion), channel_id=1, replica_groups=mesh['seg'=4,'shard'=4,'tok'=2] {'tok'}, dimensions={1}, use_global_device_ids=true | all-gather | bytes 1474560 | tf_op jit(solution)/shard_map/all_gather | solution.py:84
  475.9 3.0 copy.25
  478.9 6.6 %all-to-all-start = ((bf16[384,2,1280]{2,0,1:T(8,128)(2,1)}), bf16[384,2,1280]{2,0,1:T(8,128)(2,1)}, u32[]{:S(2)}, u32[]{:S(2)}) async-start(bf16[384,2,1280]{2,0,1:T(8,128)(2,1)} %bitcast.32), calls=%async_computation | async-start | bytes 3932160 | tf_op jit(solution)/shard_map/all_to_all | solution.py:64
  485.5 29.9 %all_gather.35 = bf16[768,512]{1,0:T(8,128)(2,1)S(1)} all-gather(bf16[384,512]{1,0:T(8,128)(2,1)S(1)} %copy-done.11), channel_id=1, replica_groups=mesh['seg'=4,'shard'=4,'tok'=2] {'tok'}, dimensions={0}, use_global_device_ids=true | all-gather | bytes 1179648 | tf_op jit(solution)/shard_map/all_gather | solution.py:63
  515.4 17.0 %psum.31 = f32[]{:T(128)} all-reduce(f32[]{:T(128)} %get-tuple-element.219), channel_id=1, replica_groups=mesh['seg'=4,'shard'=4,'tok'=2] {'shard','tok'}, use_global_device_ids=true, to_apply=%region_10.11 | all-reduce | flops 1 | bytes 8 | tf_op jit(solution)/shard_map/psum | solution.py:80
  533.1 3.7 fusion.17
  536.9 8.7 %all_gather.34 = bf16[768,512]{1,0:T(8,128)(2,1)} all-gather(bf16[384,512]{1,0:T(8,128)(2,1)S(1)} %fusion.17), channel_id=1, replica_groups=mesh['seg'=4,'shard'=4,'tok'=2] {'tok'}, dimensions={0}, use_global_device_ids=true | all-gather | bytes 1179648 | tf_op jit(solution)/shard_map/all_gather | solution.py:95
  545.6 2.2 fusion.32
  547.9 1.7 constant_dynamic-slice_fusion
  549.6 4.7 fusion.31
  (43 shorter events, 0.3 us)
Async XLA Ops:
  7.2 1.9 copy-start
  7.2 176.4 %all-reduce.4.cloned.1.call-start = ((), (), s32[]{:S(2)}) async-start(), calls=%async_computation.7 | async-start | bytes 15728640 | tf_op jit(solution)/shard_map/psum | solution.py:42
  9.1 4.8 copy-start.7
  9.1 4.8 copy-start.9
  17.5 247.1 %all-gather.7.cloned.1.call-start = ((), (), s32[]{:S(2)}) async-start(), calls=%async_computation.2 | async-start | bytes 2457600 | tf_op jit(solution)/shard_map/all_gather | solution.py:46
  183.6 45.8 %copy-start.15 = (s32[4]{0:T(128)S(1)}, s32[4]{0:T(128)}, u32[]{:S(2)}) copy-start(s32[4]{0:T(128)} %param.21) | copy-start | bytes 52
  183.6 81.1 %copy-start.12 = (f32[2560]{0:T(1024)S(1)}, f32[2560]{0:T(1024)}, u32[]{:S(2)}) copy-start(f32[2560]{0:T(1024)} %param.20) | copy-start | bytes 30724
  190.3 76.3 %copy-start.14 = (f32[512]{0:T(512)S(1)}, f32[512]{0:T(512)}, u32[]{:S(2)}) copy-start(f32[512]{0:T(512)} %param.18) | copy-start | bytes 6148
  229.3 94.7 %reduce-scatter.2.cloned.1.call-start = ((), (), s32[]{:S(2)}) async-start(), calls=%async_computation.3 | async-start | bytes 4915200 | tf_op jit(solution)/shard_map/reduce_scatter | solution.py:66
  264.6 2.3 copy-start.13
  267.0 2.6 copy-start.3
  267.0 3.3 copy-start.8
  269.6 0.8 copy-start.10
  273.4 50.8 %copy-start.4 = (bf16[384,2560]{1,0:T(8,128)(2,1)S(1)}, bf16[384,2560]{1,0:T(8,128)(2,1)}, u32[]{:S(2)}) copy-start(bf16[384,2560]{1,0:T(8,128)(2,1)} %all-gather.7.cloned.1.call-done) | copy-start | bytes 5898244
  273.4 102.8 %all-gather.11.cloned.1.call-start = ((), (), s32[]{:S(2)}) async-start(), calls=%async_computation.5 | async-start | bytes 4915200 | tf_op jit(solution)/shard_map/all_gather | solution.py:11
  324.1 119.8 %all-gather.13.cloned.1.call-start = ((), (), s32[]{:S(2)}) async-start(), calls=%async_computation.6 | async-start | bytes 4915200 | tf_op jit(solution)/shard_map/all_gather | solution.py:11
  381.8 4.8 copy-start.6
  389.7 143.5 %all-gather.9.cloned.1.call-start = ((), (), s32[]{:S(2)}) async-start(), calls=%async_computation.4 | async-start | bytes 4915200 | tf_op jit(solution)/shard_map/all_gather | solution.py:85
  453.6 4.8 copy-start.2
  475.9 9.7 %copy-start.11 = (bf16[384,512]{1,0:T(8,128)(2,1)S(1)}, bf16[384,512]{1,0:T(8,128)(2,1)}, u32[]{:S(2)}) copy-start(bf16[384,512]{1,0:T(8,128)(2,1)} %copy-done.10) | copy-start | bytes 1179652
  475.9 57.3 %copy-start.16 = (f32[384,512]{1,0:T(8,128)S(1)}, f32[384,512]{1,0:T(8,128)}, u32[]{:S(2)}) copy-start(f32[384,512]{1,0:T(8,128)} %get-tuple-element.222) | copy-start | bytes 2359300
  478.9 70.6 %all-to-all-start = ((bf16[384,2,1280]{2,0,1:T(8,128)(2,1)}), bf16[384,2,1280]{2,0,1:T(8,128)(2,1)}, u32[]{:S(2)}, u32[]{:S(2)}) async-start(bf16[384,2,1280]{2,0,1:T(8,128)(2,1)} %bitcast.32), calls=%async_computation | async-start | bytes 3932160 | tf_op jit(solution)/shard_map/all_to_all | solution.py:64
  533.1 12.5 %copy-start.5 = (bf16[2560,768]{0,1:T(8,128)(2,1)S(1)}, bf16[2560,768]{0,1:T(8,128)(2,1)}, u32[]{:S(2)}) copy-start(bf16[2560,768]{0,1:T(8,128)(2,1)} %all-gather.9.cloned.1.call-done) | copy-start | bytes 11796484
  547.9 6.4 %copy-start.1 = (bf16[640,2560]{1,0:T(8,128)(2,1)S(1)}, bf16[640,2560]{1,0:T(8,128)(2,1)}, u32[]{:S(2)}) copy-start(bf16[640,2560]{1,0:T(8,128)(2,1)} %param.14) | copy-start | bytes 9830404
Sparse Core Ops, SparseCore 0:
  17.6 165.8 all-reduce.3
  229.4 35.1 all-gather.6
  273.5 50.4 reduce-scatter.1
  325.4 50.7 all-gather.10
  389.8 53.9 all-gather.12
  476.0 50.9 all-gather.8
where the time goes:
time: 567 us; the launch traced here: 562 us
  waiting for transfers between devices  354 us (62%)
  blocking collectives  112 us (20%)
  matrix products  31.4 us (6%)
  local copies, waits for them, and re-layouts  23.8 us (4%)
  other arithmetic  17.6 us (3%)
  between operations  16.1 us (3%)
  starting transfers between devices  6.86 us (1%)
    psum x1, waiting for transfers between devices, local(): gate_total, up_total = lax.psum((gate_part, up_part), 'shard')  166 us
    all_gather x2, waiting for transfers between devices, carried_in(): pieces = lax.all_gather(value, axis)  104 us
    reduce_scatter x1, waiting for transfers between devices, local(): lax.psum_scatter(lax.dot_general(columns, latent_codes, (((0,), (1,)), ((...  50.6 us
    psum x1, blocking collectives, local(): mlp_slice = lax.psum(down_part, 'seg').astype(jnp.bfloat16)  38.9 us
    all_gather x1, waiting for transfers between devices, local(): mlp_full = lax.all_gather(mlp_slice, 'shard', axis=1, tiled=True)  34 us
    all_gather x1, blocking collectives, local(): codes_all = lax.all_gather(latent_codes, 'tok', axis=0, tiled=True)  29.9 us
    all_gather x1, blocking collectives, local(): back_all = lax.all_gather(back, 'tok', axis=1, tiled=True)  17.3 us
    psum x1, blocking collectives, local(): total_square = lax.psum(jnp.sum(errors * errors), ('shard', 'tok'))  17 us
  transfers between devices with their start and end apart: 7, of which 5 were waited for; matrix products, arithmetic and copies ran while one was open for 3% of the time, Pallas kernels for 0%

commit v1 on v0

--- a/solution.py
+++ b/solution.py
@@ -1,9 +1,18 @@
+import functools
 import math
 
 import jax
 import jax.numpy as jnp
 from jax import lax
+from jax.experimental import pallas as pl
+from jax.experimental.pallas import tpu as pltpu
 from jax.sharding import PartitionSpec as P
+
+MESH = pl.DeviceIdType.MESH
+F32 = jnp.float32
+BF16 = jnp.bfloat16
+TILE = 32
+VMEM_BYTES = 52 * 1024 * 1024
 
 
 def carried_in(value, axis, join, neutral, backward):
@@ -21,7 +30,7 @@
     return lax.fori_loop(0, count - 1, hop, subtotal)
 
 
-def local(
+def plain(
     activations,
     gate_weight,
     up_weight,
@@ -100,6 +109,510 @@
     return (grad_encoder, grad_decoder, prefix_mse)
 
 
+def send(src, dst, send_sem, recv_sem, **place):
+    return pltpu.make_async_remote_copy(
+        src_ref=src,
+        dst_ref=dst,
+        send_sem=send_sem,
+        recv_sem=recv_sem,
+        device_id=place,
+        device_id_type=MESH,
+    )
+
+
+def greet(peers):
+    barrier = pltpu.get_barrier_semaphore()
+    for place in peers:
+        pl.semaphore_signal(barrier, inc=1, device_id=place, device_id_type=MESH)
+    pl.semaphore_wait(barrier, len(peers))
+
+
+def by_rows(total, body):
+    def step(i, carry):
+        body(i * TILE)
+        return carry
+
+    lax.fori_loop(0, total // TILE, step, 0)
+
+
+def tile_at(first):
+    return pl.ds(pl.multiple_of(first, TILE), TILE)
+
+
+def span(index, size):
+    return pl.ds(pl.multiple_of(index * size, 128 if size % 128 == 0 else 32), size)
+
+
+def dot(a, b):
+    return jnp.dot(a, b, preferred_element_type=F32)
+
+
+def dot_t(a, b):
+    return lax.dot_general(a, b, (((1,), (1,)), ((), ())), preferred_element_type=F32)
+
+
+def gelu_tanh(x):
+    return x * (0.5 * (1.0 + jnp.tanh(math.sqrt(2.0 / math.pi) * (x + 0.044715 * (x * x * x)))))
+
+
+def mlp_kernel(
+    n, outer, act, wg, wu, wd, out,
+    send_a, recv_a, gate, up, hid, down, got, half, far,
+    sa, ra, sb, rb, sc, rc, sz, rz, sd, rd, se, re,
+):
+    me, sg = lax.axis_index("shard"), lax.axis_index("seg")
+    core, group = sg % 2, sg // 2
+    twin = sg + 1 - 2 * core
+    chunk = wg.shape[1] // n
+    width = wd.shape[1]
+    rows = act.shape[0]
+    part = rows // 2
+    greet(
+        [{"shard": (me + d) % n} for d in range(1, n)]
+        + [{"seg": twin}]
+        + [{"seg": ((group + d) % outer) * 2 + core} for d in range(1, outer)]
+    )
+
+    def to_peer(d, carry):
+        p = (me + d) % n
+        send_a[d - 1, :, :chunk] = dot(act[...], wg[:, span(p, chunk)]).astype(BF16)
+        send_a[d - 1, :, chunk:] = dot(act[...], wu[:, span(p, chunk)]).astype(BF16)
+        send(send_a.at[d - 1], recv_a.at[d - 1], sa.at[d - 1], ra.at[d - 1], shard=p).start()
+        return carry
+
+    lax.fori_loop(1, n, to_peer, 0)
+    gate[...] = dot(act[...], wg[:, span(me, chunk)])
+    up[...] = dot(act[...], wu[:, span(me, chunk)])
+    for d in range(1, n):
+        send(
+            send_a.at[d - 1], recv_a.at[d - 1], sa.at[d - 1], ra.at[d - 1], shard=(me + d) % n
+        ).wait()
+
+    def hidden_rows(first):
+        r = tile_at(first)
+        g, u = gate[r, :], up[r, :]
+        for d in range(n - 1):
+            g = g + recv_a[d, r, :chunk].astype(F32)
+            u = u + recv_a[d, r, chunk:].astype(F32)
+        hid[0, r, :] = (gelu_tanh(g) * u).astype(BF16)
+
+    by_rows(rows, hidden_rows)
+
+    def hid_copy(d):
+        return send(hid.at[0], hid.at[d], sb.at[d - 1], rb.at[d - 1], shard=(me + d) % n)
+
+    for d in range(1, n):
+        hid_copy(d).start()
+    down[...] = dot(hid[0], wd[span(me, chunk), :])
+
+    def from_peer(d, carry):
+        hid_copy(d).wait_recv()
+        down[...] += dot(hid[d], wd[span((me + n - d) % n, chunk), :])
+        return carry
+
+    lax.fori_loop(1, n, from_peer, 0)
+
+    core_copy = send(down.at[span(1 - core, part), :], got, sc.at[0], rc.at[0], seg=twin)
+    core_copy.start()
+    core_copy.wait()
+
+    def half_rows(first):
+        r = tile_at(first)
+        half[r, :] = (down[tile_at(core * part + first), :] + got[r, :]).astype(BF16)
+
+    by_rows(part, half_rows)
+
+    def far_copy(d):
+        to = ((group + d) % outer) * 2 + core
+        return send(half, far.at[d - 1], sz.at[d - 1], rz.at[d - 1], seg=to)
+
+    for d in range(1, outer):
+        far_copy(d).start()
+    for d in range(1, outer):
+        far_copy(d).wait()
+
+    def out_rows(first):
+        r = tile_at(first)
+        total = half[r, :].astype(F32)
+        for d in range(outer - 1):
+            total = total + far[d, r, :].astype(F32)
+        out[tile_at(core * part + first), span(me, width)] = total.astype(BF16)
+
+    by_rows(part, out_rows)
+
+    def block(c, s):
+        return out.at[span(c, part), span(s, width)]
+
+    def shard_copy(d, s):
+        return send(block(core, s), block(core, s), sd.at[d - 1], rd.at[d - 1], shard=(me + d) % n)
+
+    def twin_copy(d, c, s):
+        return send(block(c, s), block(c, s), se.at[d], re.at[d], seg=twin)
+
+    for d in range(1, n):
+        shard_copy(d, me).start()
+    twin_copy(0, core, me).start()
+    for d in range(1, n):
+        s = (me + n - d) % n
+        shard_copy(d, s).wait_recv()
+        twin_copy(d, core, s).start()
+    for d in range(n):
+        twin_copy(d, 1 - core, (me + n - d) % n).wait_recv()
+    for d in range(1, n):
+        hid_copy(d).wait_send()
+        shard_copy(d, me).wait_send()
+    for d in range(n):
+        twin_copy(d, core, (me + n - d) % n).wait_send()
+
+
+def sae_kernel(
+    n, outer, scale, count, mlp, enc, enc_bias, dec, dec_bias, live,
+    cen_out, code_out, back_out, grad_out, mse_out,
+    cen, slope, send_e, recv_e, mine, other, payload, far, back, acc, square, square_in, square_tok,
+    su, ru, sv, rv, sk, rk, sa, ra, sp, rp, sz, rz, sf, rf, sb, rb, st, rt, sg_, rg_, sm, rm, sn, rn,
+):
+    me, sg, tok = lax.axis_index("shard"), lax.axis_index("seg"), lax.axis_index("tok")
+    core, group = sg % 2, sg // 2
+    twin = sg + 1 - 2 * core
+    peer = 1 - tok
+    segments = outer * 2
+    rows, depth = mlp.shape
+    width = depth // n
+    half_width = depth // 2
+    part = rows // 2
+    per_half = n // 2
+    greet(
+        [{"shard": (me + d) % n} for d in range(1, n)]
+        + [{"seg": twin}, {"tok": peer}]
+        + [{"seg": ((group + d) % outer) * 2 + core} for d in range(1, outer)]
+    )
+
+    def center_rows(first):
+        r = tile_at(first)
+        cen[r, :] = (mlp[r, :].astype(F32) - dec_bias[...]).astype(BF16)
+        cen_out[0, r, :] = cen[r, span(tok, half_width)]
+
+    by_rows(rows, center_rows)
+
+    def cen_tok():
+        return send(
+            cen.at[span(core, part), span(peer, half_width)],
+            cen_out.at[1, span(core, part), :],
+            su.at[0], ru.at[0], tok=peer,
+        )
+
+    def cen_twin(c):
+        piece = cen_out.at[1, span(c, part), :]
+        return send(piece, piece, sv.at[0], rv.at[0], seg=twin)
+
+    cen_tok().start()
+    latents = enc.shape[1]
+    step = 256 if latents % 256 == 0 else 128
+
+    def encode(i, carry):
+        c = span(i, step)
+        pre = 10.0 * (dot(cen[...], enc[:, c]) + enc_bias[:, c])
+        on = live[:, c] > 0.0
+        soft = jnp.maximum(pre, 0.0) + jnp.log1p(jnp.exp(-jnp.abs(pre)))
+        code_out[0, :, c] = jnp.where(on, soft / 10.0, 0.0).astype(BF16)
+        slope[:, c] = jnp.where(on, jax.nn.sigmoid(pre), 0.0)
+        return carry
+
+    lax.fori_loop(0, latents // step, encode, 0)
+    code_copy = send(code_out.at[0], code_out.at[1], sk.at[0], rk.at[0], tok=peer)
+
+    def to_peer(d, carry):
+        p = (me + d) % n
+        send_e[d - 1] = dot(code_out[0], dec[:, span(p, width)]).astype(BF16)
+        send(send_e.at[d - 1], recv_e.at[d - 1], sa.at[d - 1], ra.at[d - 1], shard=p).start()
+        return carry
+
+    lax.fori_loop(1, n, to_peer, 0)
+    code_copy.start()
+    mine[...] = dot(code_out[0], dec[:, span(me, width)])
+    cen_tok().wait_recv()
+    cen_twin(core).start()
+    for d in range(1, n):
+        send(
+            send_e.at[d - 1], recv_e.at[d - 1], sa.at[d - 1], ra.at[d - 1], shard=(me + d) % n
+        ).wait()
+
+    def mine_rows(first):
+        r = tile_at(first)
+        total = mine[r, :]
+        for d in range(n - 1):
+            total = total + recv_e[d, r, :].astype(F32)
+        mine[r, :] = total
+
+    by_rows(rows, mine_rows)
+    twin_part = send(mine, other, sp.at[0], rp.at[0], seg=twin)
+    twin_part.start()
+    twin_part.wait()
+
+    def far_copy(d):
+        to = ((group + d) % outer) * 2 + core
+        piece = far.at[d - 1, span(core, part), :]
+        return send(payload.at[d - 1], piece, sz.at[d - 1], rz.at[d - 1], seg=to)
+
+    def far_twin(d, c):
+        piece = far.at[d - 1, span(c, part), :]
+        return send(piece, piece, sf.at[d - 1], rf.at[d - 1], seg=twin)
+
+    for d in range(1, outer):
+        later = (group + d) % outer > group
+        weight_mine = jnp.where(later, 1, segments - sg).astype(F32)
+        weight_other = jnp.where(later, 1, segments - twin).astype(F32)
+
+        def payload_rows(first, d=d, weight_mine=weight_mine, weight_other=weight_other):
+            q = tile_at(core * part + first)
+            payload[d - 1, tile_at(first), :] = (
+                weight_mine * mine[q, :] + weight_other * other[q, :]
+            ).astype(BF16)
+
+        by_rows(part, payload_rows)
+        far_copy(d).start()
+    for d in range(1, outer):
+        far_copy(d).wait_recv()
+        far_twin(d, core).start()
+    for d in range(1, outer):
+        far_twin(d, 1 - core).wait_recv()
+
+    ahead = (segments - sg).astype(F32)
+    other_error = core.astype(F32)
+    other_back = (segments - sg - 1 + core).astype(F32)
+    square[...] = jnp.zeros_like(square)
+    bias_here = dec_bias[:, span(me, width)]
+
+    def error_rows(first):
+        r = tile_at(first)
+        here, there = mine[r, :], other[r, :]
+        base = bias_here - mlp[r, span(me, width)].astype(F32)
+        after = jnp.zeros_like(here)
+        for d in range(1, outer):
+            before = ((group + outer - d) % outer < group).astype(F32)
+            arrived = far[d - 1, r, :].astype(F32)
+            base = base + before * arrived
+            after = after + (1.0 - before) * arrived
+        error = base + other_error * there + here
+        square[...] += error * error
+        total = ahead * (base + here) + other_back * there + after
+        back[r, span(me, width)] = (total * scale).astype(BF16)
+
+    by_rows(rows, error_rows)
+
+    def back_block(s):
+        return back.at[:, span(s, width)]
+
+    def back_copy(d, s):
+        return send(back_block(s), back_block(s), sb.at[d - 1], rb.at[d - 1], shard=(me + d) % n)
+
+    def back_tok(s, q):
+        return send(
+            back_block(s), back_out.at[1, :, span(q, width)], st.at[q], rt.at[q], tok=peer
+        )
+
+    def pass_on(s):
+        @pl.when(s // per_half == peer)
+        def _():
+            back_tok(s, s % per_half).start()
+
+    for d in range(1, n):
+        back_copy(d, me).start()
+    pass_on(me)
+    square_sum = jnp.sum(square[...]) / count
+    square_in[0] = jnp.full(square_in.shape[1:], square_sum, F32)
+
+    def square_copy(d):
+        return send(
+            square_in.at[0], square_in.at[d], sm.at[d - 1], rm.at[d - 1], shard=(me + d) % n
+        )
+
+    for d in range(1, n):
+        square_copy(d).start()
+    acc[...] = dot_t(back[:, span(me, width)], dec[:, span(me, width)])
+
+    def back_in(d, carry):
+        s = (me + n - d) % n
+        back_copy(d, s).wait_recv()
+        pass_on(s)
+        acc[...] += dot_t(back[:, span(s, width)], dec[:, span(s, width)])
+        return carry
+
+    lax.fori_loop(1, n, back_in, 0)
+
+    def grad_rows(first):
+        r = tile_at(first)
+        grad_out[0, r, :] = (acc[r, :] * slope[r, :]).astype(BF16)
+
+    by_rows(rows, grad_rows)
+    grad_copy = send(grad_out.at[0], grad_out.at[1], sg_.at[0], rg_.at[0], tok=peer)
+    grad_copy.start()
+    for d in range(1, n):
+        square_copy(d).wait()
+    total = square_in[0]
+    for d in range(1, n):
+        total = total + square_in[d]
+    square_tok[0] = total
+    tok_copy = send(square_tok.at[0], square_tok.at[1], sn.at[0], rn.at[0], tok=peer)
+    tok_copy.start()
+
+    def own_back(first):
+        r = tile_at(first)
+        back_out[0, r, :] = back[r, span(tok, half_width)]
+
+    by_rows(rows, own_back)
+    tok_copy.wait()
+    mse_out[...] = square_tok[0] + square_tok[1]
+    code_copy.wait()
+    cen_tok().wait_send()
+    cen_twin(1 - core).wait_recv()
+    cen_twin(core).wait_send()
+    for d in range(1, outer):
+        far_copy(d).wait_send()
+        far_twin(d, core).wait_send()
+    for d in range(1, n):
+        back_copy(d, me).wait_send()
+    for q in range(per_half):
+        back_tok(peer * per_half + q, q).wait()
+    grad_copy.wait()
+
+
+def vmem(count):
+    return [pl.BlockSpec(memory_space=pltpu.VMEM)] * count
+
+
+def sems(*sizes):
+    found = []
+    for size in sizes:
+        found += [pltpu.SemaphoreType.DMA((max(size, 1),))] * 2
+    return found
+
+
+def params(number):
+    return pltpu.CompilerParams(
+        collective_id=number, has_side_effects=True, vmem_limit_bytes=VMEM_BYTES
+    )
+
+
+def mlp_call(activations, gate_weight, up_weight, down_weight):
+    n, outer = lax.axis_size("shard"), lax.axis_size("seg") // 2
+    rows = activations.shape[0]
+    chunk, width = gate_weight.shape[1] // n, down_weight.shape[1]
+    part, far = rows // 2, max(outer - 1, 1)
+    return pl.pallas_call(
+        functools.partial(mlp_kernel, n, outer),
+        out_shape=jax.ShapeDtypeStruct((rows, width * n), BF16),
+        in_specs=vmem(4),
+        out_specs=vmem(1)[0],
+        scratch_shapes=[
+            pltpu.VMEM((n - 1, rows, 2 * chunk), BF16),
+            pltpu.VMEM((n - 1, rows, 2 * chunk), BF16),
+            pltpu.VMEM((rows, chunk), F32),
+            pltpu.VMEM((rows, chunk), F32),
+            pltpu.VMEM((n, rows, chunk), BF16),
+            pltpu.VMEM((rows, width), F32),
+            pltpu.VMEM((part, width), F32),
+            pltpu.VMEM((part, width), BF16),
+            pltpu.VMEM((far, part, width), BF16),
+            *sems(n - 1, n - 1, 1, outer - 1, n - 1, n),
+        ],
+        compiler_params=params(0),
+        name="mlp",
+    )(activations, gate_weight, up_weight, down_weight)
+
+
+def sae_call(mlp, enc, enc_bias, dec, dec_bias, live):
+    n, outer = lax.axis_size("shard"), lax.axis_size("seg") // 2
+    rows, depth = mlp.shape
+    width, latents = depth // n, enc.shape[1]
+    part, far, half = rows // 2, max(outer - 1, 1), depth // 2
+    tokens = rows * lax.axis_size("tok")
+    shape = jax.ShapeDtypeStruct
+    return pl.pallas_call(
+        functools.partial(sae_kernel, n, outer, 1.0 / math.sqrt(tokens), tokens * depth),
+        out_shape=(
+            shape((2, rows, half), BF16),
+            shape((2, rows, latents), BF16),
+            shape((2, rows, half), BF16),
+            shape((2, rows, latents), BF16),
+            shape((8, 128), F32),
+        ),
+        in_specs=vmem(6),
+        out_specs=tuple(vmem(5)),
+        scratch_shapes=[
+            pltpu.VMEM((rows, depth), BF16),
+            pltpu.VMEM((rows, latents), F32),
+            pltpu.VMEM((n - 1, rows, width), BF16),
+            pltpu.VMEM((n - 1, rows, width), BF16),
+            pltpu.VMEM((rows, width), F32),
+            pltpu.VMEM((rows, width), F32),
+            pltpu.VMEM((far, part, width), BF16),
+            pltpu.VMEM((far, rows, width), BF16),
+            pltpu.VMEM((rows, depth), BF16),
+            pltpu.VMEM((rows, latents), F32),
+            pltpu.VMEM((TILE, width), F32),
+            pltpu.VMEM((n, 8, 128), F32),
+            pltpu.VMEM((2, 8, 128), F32),
+            *sems(1, 1, 1, n - 1, 1, outer - 1, outer - 1, n - 1, n // 2, 1, n - 1, 1),
+        ],
+        compiler_params=params(1),
+        name="sae",
+    )(mlp, enc, enc_bias, dec, dec_bias, live)
+
+
+def fits(activations, gate_weight, encoder_weight):
+    n, segs, toks = lax.axis_size("shard"), lax.axis_size("seg"), lax.axis_size("tok")
+    rows, width = activations.shape
+    lanes = (width, gate_weight.shape[1] // n, encoder_weight.shape[1])
+    return (
+        toks == 2
+        and n % 2 == 0
+        and segs % 2 == 0
+        and rows % (2 * TILE) == 0
+        and all(size % 128 == 0 for size in lanes)
+    )
+
+
+def local(
+    activations,
+    gate_weight,
+    up_weight,
+    down_weight,
+    encoder_weight,
+    encoder_bias,
+    decoder_weight,
+    decoder_bias,
+    segment_sizes,
+):
+    if not fits(activations, gate_weight, encoder_weight):
+        return plain(
+            activations,
+            gate_weight,
+            up_weight,
+            down_weight,
+            encoder_weight,
+            encoder_bias,
+            decoder_weight,
+            decoder_bias,
+            segment_sizes,
+        )
+    latents = encoder_weight.shape[1]
+    here = jnp.arange(segment_sizes.shape[0]) == lax.axis_index("seg")
+    size_here = jnp.sum(jnp.where(here, segment_sizes, 0))
+    index = lax.axis_index("shard") * latents + jnp.arange(latents)
+    live = (index < size_here).astype(F32)[None, :]
+    mlp = mlp_call(activations, gate_weight, up_weight, down_weight)
+    cen, codes, back, code_grad, mse = sae_call(
+        mlp, encoder_weight, encoder_bias[None, :], decoder_weight, decoder_bias[None, :], live
+    )
+
+    def over_tokens(a, b):
+        a, b = (value.reshape(-1, value.shape[2]) for value in (a, b))
+        return lax.dot_general(a, b, (((0,), (0,)), ((), ())), preferred_element_type=F32)
+
+    return over_tokens(cen, code_grad), over_tokens(codes, back), mse[0, :1]
+
+
 def solution(mesh):
     in_specs = (
         P("tok", "shard"),

time: 567 us -> 225 us (0.40)
  waiting for transfers between devices: 354 us -> 0 us
  Pallas kernels: 0 us -> 213 us
  blocking collectives: 112 us -> 0 us
  matrix products: 31.4 us -> 7.09 us
  local copies, waits for them, and re-layouts: 23.8 us -> 2.26 us
  other arithmetic: 17.6 us -> 1.94 us
  between operations: 16.1 us -> 0.67 us
  starting transfers between devices: 6.86 us -> 0 us
    pallas_call x0 -> x2, Pallas kernels: none -> 213 us  [the longest x1 107 us: sae_call(): pl.pallas_call(functools.partial(sae_kernel, n, outer, 1.0 / math.sqrt(to...]
    psum x1 -> x0, waiting for transfers between devices: 166 us -> none  [local(): gate_total, up_total = lax.psum((gate_part, up_part), 'shard')]
    all_gather x4 -> x0, waiting for transfers between devices: 138 us -> none  [the longest x2 104 us: carried_in(): pieces = lax.all_gather(value, axis)]
    psum x2 -> x0, blocking collectives: 56 us -> none  [the longest x1 38.9 us: local(): mlp_slice = lax.psum(down_part, 'seg').astype(jnp.bfloat16)]
    all_gather x3 -> x0, blocking collectives: 55.9 us -> none  [the longest x1 29.9 us: local(): codes_all = lax.all_gather(latent_codes, 'tok', axis=0, tiled=True)]
    reduce_scatter x1 -> x0, waiting for transfers between devices: 50.6 us -> none  [local(): lax.psum_scatter(lax.dot_general(columns, latent_codes, (((0,), (1,)), ((...]
    dot_general x8 -> x2, matrix products: 31.4 us -> 7.09 us  [over_tokens(): lax.dot_general(a, b, (((0,), (0,)), ((), ())), preferred_element_type=F32)]
    select_n x6 -> x0, other arithmetic: 8.86 us -> none  [hop(): return jnp.where(position < mine, longer, subtotal)]
  transfers between devices with their start and end apart: 7 -> 0, of which waited for: 5 -> 0; matrix products, arithmetic and copies ran while one was open for 3% -> 0% of each run, Pallas kernels for 0% -> 0%
where the time goes in v1:
time: 225 us
  Pallas kernels  213 us (95%)
  matrix products  7.09 us (3%)
  local copies, waits for them, and re-layouts  2.26 us (1%)
    pallas_call x1, Pallas kernels, sae_call(): pl.pallas_call(functools.partial(sae_kernel, n, outer, 1.0 / math.sqrt(to...  107 us
    pallas_call x1, Pallas kernels, mlp_call(): pl.pallas_call(functools.partial(mlp_kernel, n, outer), out_shape=jax.Sha...  105 us
    dot_general x2, matrix products, over_tokens(): lax.dot_general(a, b, (((0,), (0,)), ((), ())), preferred_element_type=F32)  7.09 us

profile of v1, /device:TPU:10, one launch (start us, length us, event | category | flops | bytes accessed | tf_op | source)
XLA Modules:
  0.0 224.5 jit_solution(11648935886961458385)
XLA Ops:
  0.6 1.3 fusion
  1.9 0.7 compare_convert_fusion.live
  2.6 0.7 broadcast_in_dim.12.dec_bias
  3.3 0.0 copy-start
  3.3 1.0 copy-done
  4.3 0.0 copy-start.1
  4.3 105.3 %mlp.1 = bf16[384,2560]{1,0:T(8,128)(2,1)} custom-call(bf16[384,640]{1,0:T(8,128)(2,1)S(1)} %copy-done, bf16[640,2560]{1,0:T(8,128)(2,1)} %wg.1, bf16[640,2560]{1,0:T(8,128)(2,1)} %wu.1, bf16[2560,640]{1,0:T(8,128)(2,1)} %wd.1), custom_call_target="tpu_custom_call" | custom-call | tf_op jit(solution)/shard_map/mlp/pallas_call | solution.py:502
  109.6 0.0 copy-done.1
  109.6 107.3 %sae.1 = (bf16[2,384,1280]{2,1,0:T(8,128)(2,1)}, bf16[2,384,512]{2,1,0:T(8,128)(2,1)S(1)}, bf16[2,384,1280]{2,1,0:T(8,128)(2,1)}, bf16[2,384,512]{2,1,0:T(8,128)(2,1)S(1)}, f32[8,128]{1,0:T(8,128)S(1)}) custom-call(bf16[384,2560]{1,0:T(8,128)(2,1)} %mlp.1, bf16[2560,512]{1,0:T(8,128)(2,1)} %enc.1, f32[1,512]{1,0:T(1,128)S(1)} %bitcast.10, ...), custom_call_target="tpu_custom_call" | custom-call | tf_op jit(solution)/shard_map/sae/pallas_call | solution.py:531
  216.9 0.5 slice.3
  217.4 0.0 copy-start.2
  217.4 4.4 %convolution_bitcast_fusion.1 = f32[1280,512]{1,0:T(8,128)} fusion(bf16[2,384,1280]{2,1,0:T(8,128)(2,1)} %get-tuple-element.8, bf16[2,384,512]{2,1,0:T(8,128)(2,1)S(1)} %get-tuple-element.9), kind=kOutput, calls=%fused_computation.1 | convolution fusion | flops 1006632960 | bytes 5373952 | tf_op jit(solution)/shard_map/dot_general | solution.py:611
  221.8 0.0 copy-done.2
  221.8 2.7 %convolution_bitcast_fusion = f32[512,1280]{1,0:T(8,128)} fusion(bf16[2,384,512]{2,1,0:T(8,128)(2,1)S(1)} %get-tuple-element.10, bf16[2,384,1280]{2,1,0:T(8,128)(2,1)S(1)} %copy-done.2), kind=kOutput, calls=%fused_computation | convolution fusion | flops 1006632960 | bytes 5373952 | tf_op jit(solution)/shard_map/dot_general | solution.py:611
Async XLA Ops:
  3.3 1.0 copy-start
  4.3 105.3 %copy-start.1 = (f32[512]{0:T(512)S(1)}, f32[512]{0:T(512)}, u32[]{:S(2)}) copy-start(f32[512]{0:T(512)} %param.14) | copy-start | bytes 6148
  217.4 4.4 %copy-start.2 = (bf16[2,384,1280]{2,1,0:T(8,128)(2,1)S(1)}, bf16[2,384,1280]{2,1,0:T(8,128)(2,1)}, u32[]{:S(2)}) copy-start(bf16[2,384,1280]{2,1,0:T(8,128)(2,1)} %get-tuple-element.11) | copy-start | bytes 5898244

commit v2 on v1

--- a/solution.py
+++ b/solution.py
@@ -155,126 +155,256 @@
     return x * (0.5 * (1.0 + jnp.tanh(math.sqrt(2.0 / math.pi) * (x + 0.044715 * (x * x * x)))))
 
 
+class Links:
+    def __init__(self, send_sems, recv_sems):
+        self.sems, self.copies = (send_sems, recv_sems), {}
+
+    def start(self, number, src, dst, **place):
+        sent, got = (group.at[number] for group in self.sems)
+        self.copies[number] = send(src, dst, sent, got, **place)
+        self.copies[number].start()
+
+    def arrived(self, *numbers):
+        for number in numbers:
+            self.copies[number].wait_recv()
+
+    def finish(self):
+        for copy in self.copies.values():
+            copy.wait_send()
+
+
+def square_of(me):
+    x = me + 1 - 2 * (me % 2)
+    y = (me + 2) % 4
+    return x, y, (x + 2) % 4
+
+
+def scatter_start(links, base, fill, square, half, bufs):
+    x, y, corner = square
+    to_corner, to_x, to_y, via_x, via_y, from_x, from_y = bufs
+    top, low = pl.ds(0, half), pl.ds(half, half)
+    fill(to_corner, corner)
+    links.start(base, to_corner.at[top, :], via_x, shard=x)
+    links.start(base + 1, to_corner.at[low, :], via_y, shard=y)
+    fill(to_x, x)
+    links.start(base + 2, to_x.at[top, :], from_x.at[top, :], shard=x)
+    fill(to_y, y)
+    links.start(base + 3, to_y.at[low, :], from_y.at[low, :], shard=y)
+
+
+def scatter_forward(links, base, square, half, bufs):
+    x, y, _ = square
+    _, to_x, to_y, via_x, via_y, from_x, from_y = bufs
+    top, low = pl.ds(0, half), pl.ds(half, half)
+
+    def add_top(first):
+        r = tile_at(first)
+        to_y[r, :] = (to_y[r, :].astype(F32) + via_x[r, :].astype(F32)).astype(BF16)
+
+    def add_low(first):
+        r, q = tile_at(first), tile_at(half + first)
+        to_x[q, :] = (to_x[q, :].astype(F32) + via_y[r, :].astype(F32)).astype(BF16)
+
+    links.arrived(base)
+    by_rows(half, add_top)
+    links.start(base + 4, to_y.at[top, :], from_y.at[top, :], shard=y)
+    links.arrived(base + 1)
+    by_rows(half, add_low)
+    links.start(base + 5, to_x.at[low, :], from_x.at[low, :], shard=x)
+
+
+def scatter_wait(links, base):
+    links.arrived(base + 2, base + 3, base + 4, base + 5)
+
+
+def gather_start(links, base, block, me, square):
+    x, y, _ = square
+    links.start(base, block(me), block(me), shard=x)
+    links.start(base + 1, block(me), block(me), shard=y)
+
+
+def gather_pass_x(links, base, block, square):
+    x, y, _ = square
+    links.arrived(base)
+    links.start(base + 2, block(x, 0), block(x, 0), shard=y)
+
+
+def gather_pass_y(links, base, block, square):
+    x, y, _ = square
+    links.arrived(base + 1)
+    links.start(base + 3, block(y, 1), block(y, 1), shard=x)
+
+
 def mlp_kernel(
-    n, outer, act, wg, wu, wd, out,
-    send_a, recv_a, gate, up, hid, down, got, half, far,
-    sa, ra, sb, rb, sc, rc, sz, rz, sd, rd, se, re,
+    outer, act, wg, wu, wd, out,
+    to_corner, to_x, to_y, via_x, via_y, from_x, from_y,
+    gate, up, hid, down, got, half, far, sent, arrived,
 ):
     me, sg = lax.axis_index("shard"), lax.axis_index("seg")
     core, group = sg % 2, sg // 2
     twin = sg + 1 - 2 * core
-    chunk = wg.shape[1] // n
+    square = square_of(me)
+    x, y, corner = square
+    chunk = wg.shape[1] // 4
     width = wd.shape[1]
-    rows = act.shape[0]
+    rows = act.shape[0] // 2
     part = rows // 2
+    small = part // 2
+    links = Links(sent, arrived)
+    stride = 19 + outer - 1
     greet(
-        [{"shard": (me + d) % n} for d in range(1, n)]
-        + [{"seg": twin}]
+        [{"shard": x}, {"shard": y}, {"seg": twin}]
         + [{"seg": ((group + d) % outer) * 2 + core} for d in range(1, outer)]
     )
 
-    def to_peer(d, carry):
-        p = (me + d) % n
-        send_a[d - 1, :, :chunk] = dot(act[...], wg[:, span(p, chunk)]).astype(BF16)
-        send_a[d - 1, :, chunk:] = dot(act[...], wu[:, span(p, chunk)]).astype(BF16)
-        send(send_a.at[d - 1], recv_a.at[d - 1], sa.at[d - 1], ra.at[d - 1], shard=p).start()
-        return carry
-
-    lax.fori_loop(1, n, to_peer, 0)
-    gate[...] = dot(act[...], wg[:, span(me, chunk)])
-    up[...] = dot(act[...], wu[:, span(me, chunk)])
-    for d in range(1, n):
-        send(
-            send_a.at[d - 1], recv_a.at[d - 1], sa.at[d - 1], ra.at[d - 1], shard=(me + d) % n
-        ).wait()
-
-    def hidden_rows(first):
-        r = tile_at(first)
-        g, u = gate[r, :], up[r, :]
-        for d in range(n - 1):
-            g = g + recv_a[d, r, :chunk].astype(F32)
-            u = u + recv_a[d, r, chunk:].astype(F32)
-        hid[0, r, :] = (gelu_tanh(g) * u).astype(BF16)
-
-    by_rows(rows, hidden_rows)
-
-    def hid_copy(d):
-        return send(hid.at[0], hid.at[d], sb.at[d - 1], rb.at[d - 1], shard=(me + d) % n)
-
-    for d in range(1, n):
-        hid_copy(d).start()
-    down[...] = dot(hid[0], wd[span(me, chunk), :])
-
-    def from_peer(d, carry):
-        hid_copy(d).wait_recv()
-        down[...] += dot(hid[d], wd[span((me + n - d) % n, chunk), :])
-        return carry
-
-    lax.fori_loop(1, n, from_peer, 0)
-
-    core_copy = send(down.at[span(1 - core, part), :], got, sc.at[0], rc.at[0], seg=twin)
-    core_copy.start()
-    core_copy.wait()
-
-    def half_rows(first):
-        r = tile_at(first)
-        half[r, :] = (down[tile_at(core * part + first), :] + got[r, :]).astype(BF16)
-
-    by_rows(part, half_rows)
-
-    def far_copy(d):
-        to = ((group + d) % outer) * 2 + core
-        return send(half, far.at[d - 1], sz.at[d - 1], rz.at[d - 1], seg=to)
-
-    for d in range(1, outer):
-        far_copy(d).start()
-    for d in range(1, outer):
-        far_copy(d).wait()
-
-    def out_rows(first):
-        r = tile_at(first)
-        total = half[r, :].astype(F32)
-        for d in range(outer - 1):
-            total = total + far[d, r, :].astype(F32)
-        out[tile_at(core * part + first), span(me, width)] = total.astype(BF16)
-
-    by_rows(part, out_rows)
-
-    def block(c, s):
-        return out.at[span(c, part), span(s, width)]
-
-    def shard_copy(d, s):
-        return send(block(core, s), block(core, s), sd.at[d - 1], rd.at[d - 1], shard=(me + d) % n)
-
-    def twin_copy(d, c, s):
-        return send(block(c, s), block(c, s), se.at[d], re.at[d], seg=twin)
-
-    for d in range(1, n):
-        shard_copy(d, me).start()
-    twin_copy(0, core, me).start()
-    for d in range(1, n):
-        s = (me + n - d) % n
-        shard_copy(d, s).wait_recv()
-        twin_copy(d, core, s).start()
-    for d in range(n):
-        twin_copy(d, 1 - core, (me + n - d) % n).wait_recv()
-    for d in range(1, n):
-        hid_copy(d).wait_send()
-        shard_copy(d, me).wait_send()
-    for d in range(n):
-        twin_copy(d, core, (me + n - d) % n).wait_send()
+    def bufs(t):
+        return [b.at[t] for b in (to_corner, to_x, to_y, via_x, via_y, from_x, from_y)]
+
+    def tokens(t):
+        return act[t * rows : (t + 1) * rows, :]
+
+    def partial_start(t):
+        def fill(ref, p):
+            ref[:, :chunk] = dot(tokens(t), wg[:, span(p, chunk)]).astype(BF16)
+            ref[:, chunk:] = dot(tokens(t), wu[:, span(p, chunk)]).astype(BF16)
+
+        scatter_start(links, t * stride, fill, square, part, bufs(t))
+
+    def partial_forward(t):
+        scatter_forward(links, t * stride, square, part, bufs(t))
+
+    def partial_own(t):
+        gate[t] = dot(tokens(t), wg[:, span(me, chunk)])
+        up[t] = dot(tokens(t), wu[:, span(me, chunk)])
+
+    def hid_block(t):
+        def block(s, k=None):
+            r = pl.ds(0, rows) if k is None else pl.ds(k * part, part)
+            return hid.at[t, s, r, :]
+
+        return block
+
+    def hidden_start(t):
+        scatter_wait(links, t * stride)
+
+        def hidden_rows(first):
+            r = tile_at(first)
+            g = gate[t, r, :] + from_x[t, r, :chunk].astype(F32) + from_y[t, r, :chunk].astype(F32)
+            u = up[t, r, :] + from_x[t, r, chunk:].astype(F32) + from_y[t, r, chunk:].astype(F32)
+            hid[t, me, r, :] = (gelu_tanh(g) * u).astype(BF16)
+
+        by_rows(rows, hidden_rows)
+        gather_start(links, t * stride + 6, hid_block(t), me, square)
+
+    def hidden_forward(t):
+        gather_pass_x(links, t * stride + 6, hid_block(t), square)
+        gather_pass_y(links, t * stride + 6, hid_block(t), square)
+
+    def term(t, s):
+        return dot(hid[t, s], wd[span(s, chunk), :])
+
+    def down_near(t):
+        down[t] = term(t, me) + term(t, x) + term(t, y)
+
+    def down_start(t):
+        links.arrived(t * stride + 8, t * stride + 9)
+        down[t] += term(t, corner)
+        links.start(t * stride + 10, down.at[t, span(1 - core, part), :], got.at[t], seg=twin)
+
+    def far_start(t):
+        links.arrived(t * stride + 10)
+
+        def half_rows(first):
+            r = tile_at(first)
+            half[t, r, :] = (down[t, tile_at(core * part + first), :] + got[t, r, :]).astype(BF16)
+
+        by_rows(part, half_rows)
+        for d in range(1, outer):
+            to = ((group + d) % outer) * 2 + core
+            links.start(t * stride + 18 + d, half.at[t], far.at[t, d - 1], seg=to)
+
+    def out_block(t):
+        def block(s, k=None):
+            first = t * rows + core * part
+            if k is None:
+                r = pl.ds(pl.multiple_of(first, 32), part)
+            else:
+                r = pl.ds(pl.multiple_of(first + k * small, 16), small)
+            return out.at[r, span(s, width)]
+
+        return block
+
+    def twin_start(t, number, s):
+        piece = out_block(t)(s)
+        links.start(t * stride + 15 + number, piece, piece, seg=twin)
+
+    def out_start(t):
+        for d in range(1, outer):
+            links.arrived(t * stride + 18 + d)
+
+        def out_rows(first):
+            r = tile_at(first)
+            total = half[t, r, :].astype(F32)
+            for d in range(outer - 1):
+                total = total + far[t, d, r, :].astype(F32)
+            out[tile_at(t * rows + core * part + first), span(me, width)] = total.astype(BF16)
+
+        by_rows(part, out_rows)
+        gather_start(links, t * stride + 11, out_block(t), me, square)
+        twin_start(t, 0, me)
+
+    def out_forward(t):
+        gather_pass_x(links, t * stride + 11, out_block(t), square)
+        twin_start(t, 1, x)
+        gather_pass_y(links, t * stride + 11, out_block(t), square)
+        twin_start(t, 2, y)
+
+    def out_last(t):
+        links.arrived(t * stride + 13, t * stride + 14)
+        twin_start(t, 3, corner)
+
+    partial_start(0)
+    partial_forward(0)
+    partial_start(1)
+    partial_own(0)
+    hidden_start(0)
+    partial_forward(1)
+    partial_own(1)
+    hidden_forward(0)
+    down_near(0)
+    hidden_start(1)
+    down_start(0)
+    far_start(0)
+    hidden_forward(1)
+    down_near(1)
+    out_start(0)
+    down_start(1)
+    far_start(1)
+    out_forward(0)
+    out_last(0)
+    out_start(1)
+    out_forward(1)
+    out_last(1)
+    for t in range(2):
+        links.arrived(*(t * stride + 15 + k for k in range(4)))
+    links.finish()
 
 
 def sae_kernel(
-    n, outer, scale, count, mlp, enc, enc_bias, dec, dec_bias, live,
+    outer, scale, count, mlp, enc, enc_bias, dec, dec_bias, live,
     cen_out, code_out, back_out, grad_out, mse_out,
-    cen, slope, send_e, recv_e, mine, other, payload, far, back, acc, square, square_in, square_tok,
-    su, ru, sv, rv, sk, rk, sa, ra, sp, rp, sz, rz, sf, rf, sb, rb, st, rt, sg_, rg_, sm, rm, sn, rn,
+    cen, slope, to_corner, to_x, to_y, via_x, via_y, from_x, from_y, mine, other, payload, far, back, acc, squares, square_in, square_tok,
+    sent, arrived,
+    su, ru, sv, rv, sk, rk, sp, rp, sz, rz, sf, rf, st, rt, sg_, rg_, sn, rn,
 ):
     me, sg, tok = lax.axis_index("shard"), lax.axis_index("seg"), lax.axis_index("tok")
     core, group = sg % 2, sg // 2
     twin = sg + 1 - 2 * core
     peer = 1 - tok
+    square = square_of(me)
+    x, y, corner = square
+    links = Links(sent, arrived)
+    n = 4
     segments = outer * 2
     rows, depth = mlp.shape
     width = depth // n
@@ -282,8 +412,7 @@
     part = rows // 2
     per_half = n // 2
     greet(
-        [{"shard": (me + d) % n} for d in range(1, n)]
-        + [{"seg": twin}, {"tok": peer}]
+        [{"shard": x}, {"shard": y}, {"seg": twin}, {"tok": peer}]
         + [{"seg": ((group + d) % outer) * 2 + core} for d in range(1, outer)]
     )
 
@@ -321,28 +450,22 @@
     lax.fori_loop(0, latents // step, encode, 0)
     code_copy = send(code_out.at[0], code_out.at[1], sk.at[0], rk.at[0], tok=peer)
 
-    def to_peer(d, carry):
-        p = (me + d) % n
-        send_e[d - 1] = dot(code_out[0], dec[:, span(p, width)]).astype(BF16)
-        send(send_e.at[d - 1], recv_e.at[d - 1], sa.at[d - 1], ra.at[d - 1], shard=p).start()
-        return carry
-
-    lax.fori_loop(1, n, to_peer, 0)
+    bufs = (to_corner, to_x, to_y, via_x, via_y, from_x, from_y)
+
+    def fill(ref, p):
+        ref[...] = dot(code_out[0], dec[:, span(p, width)]).astype(BF16)
+
+    scatter_start(links, 0, fill, square, part, bufs)
     code_copy.start()
     mine[...] = dot(code_out[0], dec[:, span(me, width)])
+    scatter_forward(links, 0, square, part, bufs)
     cen_tok().wait_recv()
     cen_twin(core).start()
-    for d in range(1, n):
-        send(
-            send_e.at[d - 1], recv_e.at[d - 1], sa.at[d - 1], ra.at[d - 1], shard=(me + d) % n
-        ).wait()
+    scatter_wait(links, 0)
 
     def mine_rows(first):
         r = tile_at(first)
-        total = mine[r, :]
-        for d in range(n - 1):
-            total = total + recv_e[d, r, :].astype(F32)
-        mine[r, :] = total
+        mine[r, :] = mine[r, :] + from_x[r, :].astype(F32) + from_y[r, :].astype(F32)
 
     by_rows(rows, mine_rows)
     twin_part = send(mine, other, sp.at[0], rp.at[0], seg=twin)
@@ -380,7 +503,7 @@
     ahead = (segments - sg).astype(F32)
     other_error = core.astype(F32)
     other_back = (segments - sg - 1 + core).astype(F32)
-    square[...] = jnp.zeros_like(square)
+    squares[...] = jnp.zeros_like(squares)
     bias_here = dec_bias[:, span(me, width)]
 
     def error_rows(first):
@@ -394,17 +517,15 @@
             base = base + before * arrived
             after = after + (1.0 - before) * arrived
         error = base + other_error * there + here
-        square[...] += error * error
+        squares[...] += error * error
         total = ahead * (base + here) + other_back * there + after
         back[r, span(me, width)] = (total * scale).astype(BF16)
 
     by_rows(rows, error_rows)
 
-    def back_block(s):
-        return back.at[:, span(s, width)]
-
-    def back_copy(d, s):
-        return send(back_block(s), back_block(s), sb.at[d - 1], rb.at[d - 1], shard=(me + d) % n)
+    def back_block(s, k=None):
+        r = pl.ds(0, rows) if k is None else pl.ds(k * part, part)
+        return back.at[r, span(s, width)]
 
     def back_tok(s, q):
         return send(
@@ -416,29 +537,26 @@
         def _():
             back_tok(s, s % per_half).start()
 
-    for d in range(1, n):
-        back_copy(d, me).start()
+    def back_term(s):
+        return dot_t(back[:, span(s, width)], dec[:, span(s, width)])
+
+    gather_start(links, 6, back_block, me, square)
     pass_on(me)
-    square_sum = jnp.sum(square[...]) / count
+    square_sum = jnp.sum(squares[...]) / count
     square_in[0] = jnp.full(square_in.shape[1:], square_sum, F32)
-
-    def square_copy(d):
-        return send(
-            square_in.at[0], square_in.at[d], sm.at[d - 1], rm.at[d - 1], shard=(me + d) % n
-        )
-
-    for d in range(1, n):
-        square_copy(d).start()
-    acc[...] = dot_t(back[:, span(me, width)], dec[:, span(me, width)])
-
-    def back_in(d, carry):
-        s = (me + n - d) % n
-        back_copy(d, s).wait_recv()
-        pass_on(s)
-        acc[...] += dot_t(back[:, span(s, width)], dec[:, span(s, width)])
-        return carry
-
-    lax.fori_loop(1, n, back_in, 0)
+    links.start(10, square_in.at[0], square_in.at[1], shard=x)
+    acc[...] = back_term(me)
+    gather_pass_x(links, 6, back_block, square)
+    pass_on(x)
+    gather_pass_y(links, 6, back_block, square)
+    pass_on(y)
+    links.arrived(10)
+    square_in[2] = square_in[0] + square_in[1]
+    links.start(11, square_in.at[2], square_in.at[3], shard=y)
+    acc[...] += back_term(x) + back_term(y)
+    links.arrived(8, 9)
+    pass_on(corner)
+    acc[...] += back_term(corner)
 
     def grad_rows(first):
         r = tile_at(first)
@@ -447,12 +565,8 @@
     by_rows(rows, grad_rows)
     grad_copy = send(grad_out.at[0], grad_out.at[1], sg_.at[0], rg_.at[0], tok=peer)
     grad_copy.start()
-    for d in range(1, n):
-        square_copy(d).wait()
-    total = square_in[0]
-    for d in range(1, n):
-        total = total + square_in[d]
-    square_tok[0] = total
+    links.arrived(11)
+    square_tok[0] = square_in[2] + square_in[3]
     tok_copy = send(square_tok.at[0], square_tok.at[1], sn.at[0], rn.at[0], tok=peer)
     tok_copy.start()
 
@@ -470,8 +584,7 @@
     for d in range(1, outer):
         far_copy(d).wait_send()
         far_twin(d, core).wait_send()
-    for d in range(1, n):
-        back_copy(d, me).wait_send()
+    links.finish()
     for q in range(per_half):
         back_tok(peer * per_half + q, q).wait()
     grad_copy.wait()
@@ -494,27 +607,31 @@
     )
 
 
+def scatter_bufs(lead, rows, width):
+    whole, half = lead + (rows, width), lead + (rows // 2, width)
+    return [pltpu.VMEM(shape, BF16) for shape in (whole,) * 3 + (half,) * 2 + (whole,) * 2]
+
+
 def mlp_call(activations, gate_weight, up_weight, down_weight):
     n, outer = lax.axis_size("shard"), lax.axis_size("seg") // 2
-    rows = activations.shape[0]
+    tokens = activations.shape[0]
     chunk, width = gate_weight.shape[1] // n, down_weight.shape[1]
-    part, far = rows // 2, max(outer - 1, 1)
+    rows, part, far = tokens // 2, tokens // 4, max(outer - 1, 1)
     return pl.pallas_call(
-        functools.partial(mlp_kernel, n, outer),
-        out_shape=jax.ShapeDtypeStruct((rows, width * n), BF16),
+        functools.partial(mlp_kernel, outer),
+        out_shape=jax.ShapeDtypeStruct((tokens, width * n), BF16),
         in_specs=vmem(4),
         out_specs=vmem(1)[0],
         scratch_shapes=[
-            pltpu.VMEM((n - 1, rows, 2 * chunk), BF16),
-            pltpu.VMEM((n - 1, rows, 2 * chunk), BF16),
-            pltpu.VMEM((rows, chunk), F32),
-            pltpu.VMEM((rows, chunk), F32),
-            pltpu.VMEM((n, rows, chunk), BF16),
-            pltpu.VMEM((rows, width), F32),
-            pltpu.VMEM((part, width), F32),
-            pltpu.VMEM((part, width), BF16),
-            pltpu.VMEM((far, part, width), BF16),
-            *sems(n - 1, n - 1, 1, outer - 1, n - 1, n),
+            *scatter_bufs((2,), rows, 2 * chunk),
+            pltpu.VMEM((2, rows, chunk), F32),
+            pltpu.VMEM((2, rows, chunk), F32),
+            pltpu.VMEM((2, n, rows, chunk), BF16),
+            pltpu.VMEM((2, rows, width), F32),
+            pltpu.VMEM((2, part, width), F32),
+            pltpu.VMEM((2, part, width), BF16),
+            pltpu.VMEM((2, far, part, width), BF16),
+            *sems(2 * (18 + outer)),
         ],
         compiler_params=params(0),
         name="mlp",
@@ -529,7 +646,7 @@
     tokens = rows * lax.axis_size("tok")
     shape = jax.ShapeDtypeStruct
     return pl.pallas_call(
-        functools.partial(sae_kernel, n, outer, 1.0 / math.sqrt(tokens), tokens * depth),
+        functools.partial(sae_kernel, outer, 1.0 / math.sqrt(tokens), tokens * depth),
         out_shape=(
             shape((2, rows, half), BF16),
             shape((2, rows, latents), BF16),
@@ -542,8 +659,7 @@
         scratch_shapes=[
             pltpu.VMEM((rows, depth), BF16),
             pltpu.VMEM((rows, latents), F32),
-            pltpu.VMEM((n - 1, rows, width), BF16),
-            pltpu.VMEM((n - 1, rows, width), BF16),
+            *scatter_bufs((), rows, width),
             pltpu.VMEM((rows, width), F32),
             pltpu.VMEM((rows, width), F32),
             pltpu.VMEM((far, part, width), BF16),
@@ -553,7 +669,7 @@
             pltpu.VMEM((TILE, width), F32),
             pltpu.VMEM((n, 8, 128), F32),
             pltpu.VMEM((2, 8, 128), F32),
-            *sems(1, 1, 1, n - 1, 1, outer - 1, outer - 1, n - 1, n // 2, 1, n - 1, 1),
+            *sems(12, 1, 1, 1, 1, outer - 1, outer - 1, n // 2, 1, 1),
         ],
         compiler_params=params(1),
         name="sae",
@@ -566,9 +682,9 @@
     lanes = (width, gate_weight.shape[1] // n, encoder_weight.shape[1])
     return (
         toks == 2
-        and n % 2 == 0
+        and n == 4
         and segs % 2 == 0
-        and rows % (2 * TILE) == 0
+        and rows % (4 * TILE) == 0
         and all(size % 128 == 0 for size in lanes)
     )
 

time: 225 us -> 180 us (0.80)
  Pallas kernels: 213 us -> 167 us
    pallas_call x2, Pallas kernels: 213 us -> 167 us  [the longest x1 91.1 us: sae_call(): pl.pallas_call(functools.partial(sae_kernel, outer, 1.0 / math.sqrt(token...]
where the time goes in v2:
time: 180 us; the launch traced here: 179 us
  Pallas kernels  167 us (93%)
  matrix products  7.09 us (4%)
  local copies, waits for them, and re-layouts  2.26 us (1%)
  other arithmetic  1.94 us (1%)
    pallas_call x1, Pallas kernels, sae_call(): pl.pallas_call(functools.partial(sae_kernel, outer, 1.0 / math.sqrt(token...  91.1 us
    pallas_call x1, Pallas kernels, mlp_call(): pl.pallas_call(functools.partial(mlp_kernel, outer), out_shape=jax.ShapeD...  75.7 us
    dot_general x2, matrix products, over_tokens(): lax.dot_general(a, b, (((0,), (0,)), ((), ())), preferred_element_type=F32)  7.09 us

profile of v2, /device:TPU:10, one launch (start us, length us, event | category | flops | bytes accessed | tf_op | source)
XLA Modules:
  0.0 178.8 jit_solution(7804481841571857360)
XLA Ops:
  0.6 1.3 fusion
  1.9 0.7 compare_convert_fusion.live
  2.6 0.7 broadcast_in_dim.12.dec_bias
  3.3 0.0 copy-start
  3.3 1.0 copy-done
  4.3 0.0 copy-start.1
  4.3 75.7 %mlp.1 = bf16[384,2560]{1,0:T(8,128)(2,1)} custom-call(bf16[384,640]{1,0:T(8,128)(2,1)S(1)} %copy-done, bf16[640,2560]{1,0:T(8,128)(2,1)} %wg.1, bf16[640,2560]{1,0:T(8,128)(2,1)} %wu.1, bf16[2560,640]{1,0:T(8,128)(2,1)} %wd.1), custom_call_target="tpu_custom_call" | custom-call | tf_op jit(solution)/shard_map/mlp/pallas_call | solution.py:620
  80.1 0.0 copy-done.1
  80.1 91.1 %sae.1 = (bf16[2,384,1280]{2,1,0:T(8,128)(2,1)}, bf16[2,384,512]{2,1,0:T(8,128)(2,1)S(1)}, bf16[2,384,1280]{2,1,0:T(8,128)(2,1)}, bf16[2,384,512]{2,1,0:T(8,128)(2,1)S(1)}, f32[8,128]{1,0:T(8,128)S(1)}) custom-call(bf16[384,2560]{1,0:T(8,128)(2,1)} %mlp.1, bf16[2560,512]{1,0:T(8,128)(2,1)} %enc.1, f32[1,512]{1,0:T(1,128)S(1)} %bitcast.10, ...), custom_call_target="tpu_custom_call" | custom-call | tf_op jit(solution)/shard_map/sae/pallas_call | solution.py:648
  171.2 0.5 slice.3
  171.7 0.0 copy-start.2
  171.7 4.4 %convolution_bitcast_fusion.1 = f32[1280,512]{1,0:T(8,128)} fusion(bf16[2,384,1280]{2,1,0:T(8,128)(2,1)} %get-tuple-element.8, bf16[2,384,512]{2,1,0:T(8,128)(2,1)S(1)} %get-tuple-element.9), kind=kOutput, calls=%fused_computation.1 | convolution fusion | flops 1006632960 | bytes 5373952 | tf_op jit(solution)/shard_map/dot_general | solution.py:727
  176.1 0.0 copy-done.2
  176.1 2.7 %convolution_bitcast_fusion = f32[512,1280]{1,0:T(8,128)} fusion(bf16[2,384,512]{2,1,0:T(8,128)(2,1)S(1)} %get-tuple-element.10, bf16[2,384,1280]{2,1,0:T(8,128)(2,1)S(1)} %copy-done.2), kind=kOutput, calls=%fused_computation | convolution fusion | flops 1006632960 | bytes 5373952 | tf_op jit(solution)/shard_map/dot_general | solution.py:727
Async XLA Ops:
  3.3 1.0 copy-start
  4.3 75.7 %copy-start.1 = (f32[512]{0:T(512)S(1)}, f32[512]{0:T(512)}, u32[]{:S(2)}) copy-start(f32[512]{0:T(512)} %param.14) | copy-start | bytes 6148
  171.7 4.4 %copy-start.2 = (bf16[2,384,1280]{2,1,0:T(8,128)(2,1)S(1)}, bf16[2,384,1280]{2,1,0:T(8,128)(2,1)}, u32[]{:S(2)}) copy-start(bf16[2,384,1280]{2,1,0:T(8,128)(2,1)} %get-tuple-element.11) | copy-start | bytes 5898244

commit v3 on v2

--- a/solution.py
+++ b/solution.py
@@ -393,9 +393,8 @@
 def sae_kernel(
     outer, scale, count, mlp, enc, enc_bias, dec, dec_bias, live,
     cen_out, code_out, back_out, grad_out, mse_out,
-    cen, slope, to_corner, to_x, to_y, via_x, via_y, from_x, from_y, mine, other, payload, far, back, acc, squares, square_in, square_tok,
-    sent, arrived,
-    su, ru, sv, rv, sk, rk, sp, rp, sz, rz, sf, rf, st, rt, sg_, rg_, sn, rn,
+    cen, slope, to_corner, to_x, to_y, via_x, via_y, from_x, from_y, mine, other, payload, far,
+    back, acc, squares, square_in, square_tok, sent, arrived, back_sent, back_arrived,
 ):
     me, sg, tok = lax.axis_index("shard"), lax.axis_index("seg"), lax.axis_index("tok")
     core, group = sg % 2, sg // 2
@@ -404,13 +403,16 @@
     square = square_of(me)
     x, y, corner = square
     links = Links(sent, arrived)
-    n = 4
     segments = outer * 2
-    rows, depth = mlp.shape
-    width = depth // n
+    tokens, depth = mlp.shape
+    width = depth // 4
     half_width = depth // 2
+    rows = tokens // 2
     part = rows // 2
-    per_half = n // 2
+    stride = 12 + 2 * (outer - 1)
+    code_link, cen_link, cen_twin, near_square, far_square, tok_square = (
+        2 * stride + k for k in range(6)
+    )
     greet(
         [{"shard": x}, {"shard": y}, {"seg": twin}, {"tok": peer}]
         + [{"seg": ((group + d) % outer) * 2 + core} for d in range(1, outer)]
@@ -421,173 +423,218 @@
         cen[r, :] = (mlp[r, :].astype(F32) - dec_bias[...]).astype(BF16)
         cen_out[0, r, :] = cen[r, span(tok, half_width)]
 
-    by_rows(rows, center_rows)
-
-    def cen_tok():
-        return send(
-            cen.at[span(core, part), span(peer, half_width)],
-            cen_out.at[1, span(core, part), :],
-            su.at[0], ru.at[0], tok=peer,
-        )
-
-    def cen_twin(c):
-        piece = cen_out.at[1, span(c, part), :]
-        return send(piece, piece, sv.at[0], rv.at[0], seg=twin)
-
-    cen_tok().start()
+    def bufs(t):
+        return [b.at[t] for b in (to_corner, to_x, to_y, via_x, via_y, from_x, from_y)]
+
+    def half_of(t):
+        return pl.ds(t * rows, rows)
+
     latents = enc.shape[1]
     step = 256 if latents % 256 == 0 else 128
 
-    def encode(i, carry):
-        c = span(i, step)
-        pre = 10.0 * (dot(cen[...], enc[:, c]) + enc_bias[:, c])
-        on = live[:, c] > 0.0
-        soft = jnp.maximum(pre, 0.0) + jnp.log1p(jnp.exp(-jnp.abs(pre)))
-        code_out[0, :, c] = jnp.where(on, soft / 10.0, 0.0).astype(BF16)
-        slope[:, c] = jnp.where(on, jax.nn.sigmoid(pre), 0.0)
-        return carry
-
-    lax.fori_loop(0, latents // step, encode, 0)
-    code_copy = send(code_out.at[0], code_out.at[1], sk.at[0], rk.at[0], tok=peer)
-
-    bufs = (to_corner, to_x, to_y, via_x, via_y, from_x, from_y)
-
-    def fill(ref, p):
-        ref[...] = dot(code_out[0], dec[:, span(p, width)]).astype(BF16)
-
-    scatter_start(links, 0, fill, square, part, bufs)
-    code_copy.start()
-    mine[...] = dot(code_out[0], dec[:, span(me, width)])
-    scatter_forward(links, 0, square, part, bufs)
-    cen_tok().wait_recv()
-    cen_twin(core).start()
-    scatter_wait(links, 0)
-
-    def mine_rows(first):
-        r = tile_at(first)
-        mine[r, :] = mine[r, :] + from_x[r, :].astype(F32) + from_y[r, :].astype(F32)
-
-    by_rows(rows, mine_rows)
-    twin_part = send(mine, other, sp.at[0], rp.at[0], seg=twin)
-    twin_part.start()
-    twin_part.wait()
-
-    def far_copy(d):
-        to = ((group + d) % outer) * 2 + core
-        piece = far.at[d - 1, span(core, part), :]
-        return send(payload.at[d - 1], piece, sz.at[d - 1], rz.at[d - 1], seg=to)
-
-    def far_twin(d, c):
-        piece = far.at[d - 1, span(c, part), :]
-        return send(piece, piece, sf.at[d - 1], rf.at[d - 1], seg=twin)
-
-    for d in range(1, outer):
-        later = (group + d) % outer > group
-        weight_mine = jnp.where(later, 1, segments - sg).astype(F32)
-        weight_other = jnp.where(later, 1, segments - twin).astype(F32)
-
-        def payload_rows(first, d=d, weight_mine=weight_mine, weight_other=weight_other):
-            q = tile_at(core * part + first)
-            payload[d - 1, tile_at(first), :] = (
-                weight_mine * mine[q, :] + weight_other * other[q, :]
-            ).astype(BF16)
-
-        by_rows(part, payload_rows)
-        far_copy(d).start()
-    for d in range(1, outer):
-        far_copy(d).wait_recv()
-        far_twin(d, core).start()
-    for d in range(1, outer):
-        far_twin(d, 1 - core).wait_recv()
+    def encode(t):
+        def columns(i, carry):
+            c = span(i, step)
+            pre = 10.0 * (dot(cen[half_of(t), :], enc[:, c]) + enc_bias[:, c])
+            on = live[:, c] > 0.0
+            soft = jnp.maximum(pre, 0.0) + jnp.log1p(jnp.exp(-jnp.abs(pre)))
+            code_out[0, half_of(t), c] = jnp.where(on, soft / 10.0, 0.0).astype(BF16)
+            slope[half_of(t), c] = jnp.where(on, jax.nn.sigmoid(pre), 0.0)
+            return carry
+
+        lax.fori_loop(0, latents // step, columns, 0)
+
+    def part_start(t):
+        def fill(ref, p):
+            ref[...] = dot(code_out[0, half_of(t), :], dec[:, span(p, width)]).astype(BF16)
+
+        scatter_start(links, t * stride, fill, square, part, bufs(t))
+
+    def part_forward(t):
+        scatter_forward(links, t * stride, square, part, bufs(t))
+
+    def part_own(t):
+        mine[half_of(t), :] = dot(code_out[0, half_of(t), :], dec[:, span(me, width)])
+
+    def part_sum(t):
+        scatter_wait(links, t * stride)
+
+        def mine_rows(first):
+            r, q = tile_at(first), tile_at(t * rows + first)
+            mine[q, :] = mine[q, :] + from_x[t, r, :].astype(F32) + from_y[t, r, :].astype(F32)
+
+        by_rows(rows, mine_rows)
+        links.start(
+            t * stride + 10, mine.at[half_of(t), :], other.at[half_of(t), :], seg=twin
+        )
+
+    def core_rows(t):
+        return pl.ds(pl.multiple_of(t * rows + core * part, TILE), part)
+
+    def far_start(t):
+        links.arrived(t * stride + 10)
+        for d in range(1, outer):
+            to = (group + d) % outer
+            later = to > group
+            weight_mine = jnp.where(later, 1, segments - sg).astype(F32)
+            weight_other = jnp.where(later, 1, segments - twin).astype(F32)
+
+            def payload_rows(first, d=d, weight_mine=weight_mine, weight_other=weight_other):
+                q = tile_at(t * rows + core * part + first)
+                payload[t, d - 1, tile_at(first), :] = (
+                    weight_mine * mine[q, :] + weight_other * other[q, :]
+                ).astype(BF16)
+
+            by_rows(part, payload_rows)
+            links.start(
+                t * stride + 11 + d,
+                payload.at[t, d - 1],
+                far.at[d - 1, core_rows(t), :],
+                seg=to * 2 + core,
+            )
+
+    def far_pass(t):
+        for d in range(1, outer):
+            links.arrived(t * stride + 11 + d)
+            piece = far.at[d - 1, core_rows(t), :]
+            links.start(t * stride + 10 + outer + d, piece, piece, seg=twin)
 
     ahead = (segments - sg).astype(F32)
     other_error = core.astype(F32)
     other_back = (segments - sg - 1 + core).astype(F32)
+    bias_here = dec_bias[:, span(me, width)]
+
+    def back_block(t):
+        def block(s, k=None):
+            r = half_of(t) if k is None else pl.ds(t * rows + k * part, part)
+            return back.at[r, span(s, width)]
+
+        return block
+
+    def back_tok(t, s):
+        q = s % 2
+        return send(
+            back_block(t)(s),
+            back_out.at[1, half_of(t), span(q, width)],
+            back_sent.at[t * 2 + q],
+            back_arrived.at[t * 2 + q],
+            tok=peer,
+        )
+
+    def pass_on(t, s):
+        @pl.when(s // 2 == peer)
+        def _():
+            back_tok(t, s).start()
+
+    def back_start(t):
+        for d in range(1, outer):
+            links.arrived(t * stride + 10 + outer + d)
+
+        def error_rows(first):
+            r = tile_at(t * rows + first)
+            here, there = mine[r, :], other[r, :]
+            base = bias_here - mlp[r, span(me, width)].astype(F32)
+            after = jnp.zeros_like(here)
+            for d in range(1, outer):
+                before = ((group + outer - d) % outer < group).astype(F32)
+                came = far[d - 1, r, :].astype(F32)
+                base = base + before * came
+                after = after + (1.0 - before) * came
+            error = base + other_error * there + here
+            squares[...] += error * error
+            total = ahead * (base + here) + other_back * there + after
+            back[r, span(me, width)] = (total * scale).astype(BF16)
+
+        by_rows(rows, error_rows)
+        gather_start(links, t * stride + 6, back_block(t), me, square)
+        pass_on(t, me)
+
+    def back_term(t, s):
+        return dot_t(back[half_of(t), span(s, width)], dec[:, span(s, width)])
+
+    def back_forward(t):
+        gather_pass_x(links, t * stride + 6, back_block(t), square)
+        pass_on(t, x)
+        gather_pass_y(links, t * stride + 6, back_block(t), square)
+        pass_on(t, y)
+
+    def back_near(t):
+        acc[half_of(t), :] = back_term(t, me) + back_term(t, x) + back_term(t, y)
+
+    def back_last(t):
+        links.arrived(t * stride + 8, t * stride + 9)
+        pass_on(t, corner)
+        acc[half_of(t), :] += back_term(t, corner)
+
+        def grad_rows(first):
+            r = tile_at(t * rows + first)
+            grad_out[0, r, :] = (acc[r, :] * slope[r, :]).astype(BF16)
+
+        by_rows(rows, grad_rows)
+        links.start(
+            t * stride + 11,
+            grad_out.at[0, half_of(t), :],
+            grad_out.at[1, half_of(t), :],
+            tok=peer,
+        )
+
     squares[...] = jnp.zeros_like(squares)
-    bias_here = dec_bias[:, span(me, width)]
-
-    def error_rows(first):
-        r = tile_at(first)
-        here, there = mine[r, :], other[r, :]
-        base = bias_here - mlp[r, span(me, width)].astype(F32)
-        after = jnp.zeros_like(here)
-        for d in range(1, outer):
-            before = ((group + outer - d) % outer < group).astype(F32)
-            arrived = far[d - 1, r, :].astype(F32)
-            base = base + before * arrived
-            after = after + (1.0 - before) * arrived
-        error = base + other_error * there + here
-        squares[...] += error * error
-        total = ahead * (base + here) + other_back * there + after
-        back[r, span(me, width)] = (total * scale).astype(BF16)
-
-    by_rows(rows, error_rows)
-
-    def back_block(s, k=None):
-        r = pl.ds(0, rows) if k is None else pl.ds(k * part, part)
-        return back.at[r, span(s, width)]
-
-    def back_tok(s, q):
-        return send(
-            back_block(s), back_out.at[1, :, span(q, width)], st.at[q], rt.at[q], tok=peer
-        )
-
-    def pass_on(s):
-        @pl.when(s // per_half == peer)
-        def _():
-            back_tok(s, s % per_half).start()
-
-    def back_term(s):
-        return dot_t(back[:, span(s, width)], dec[:, span(s, width)])
-
-    gather_start(links, 6, back_block, me, square)
-    pass_on(me)
+    by_rows(tokens, center_rows)
+    encode(0)
+    part_start(0)
+    links.start(
+        cen_link,
+        cen.at[span(core, rows), span(peer, half_width)],
+        cen_out.at[1, span(core, rows), :],
+        tok=peer,
+    )
+    encode(1)
+    part_forward(0)
+    part_start(1)
+    part_own(0)
+    part_sum(0)
+    part_forward(1)
+    far_start(0)
+    part_own(1)
+    links.start(code_link, code_out.at[0], code_out.at[1], tok=peer)
+    far_pass(0)
+    part_sum(1)
+    back_start(0)
+    far_start(1)
+    back_forward(0)
+    far_pass(1)
+    back_near(0)
+    back_start(1)
+    back_last(0)
     square_sum = jnp.sum(squares[...]) / count
     square_in[0] = jnp.full(square_in.shape[1:], square_sum, F32)
-    links.start(10, square_in.at[0], square_in.at[1], shard=x)
-    acc[...] = back_term(me)
-    gather_pass_x(links, 6, back_block, square)
-    pass_on(x)
-    gather_pass_y(links, 6, back_block, square)
-    pass_on(y)
-    links.arrived(10)
+    links.start(near_square, square_in.at[0], square_in.at[1], shard=x)
+    back_forward(1)
+    back_near(1)
+    links.arrived(near_square)
     square_in[2] = square_in[0] + square_in[1]
-    links.start(11, square_in.at[2], square_in.at[3], shard=y)
-    acc[...] += back_term(x) + back_term(y)
-    links.arrived(8, 9)
-    pass_on(corner)
-    acc[...] += back_term(corner)
-
-    def grad_rows(first):
-        r = tile_at(first)
-        grad_out[0, r, :] = (acc[r, :] * slope[r, :]).astype(BF16)
-
-    by_rows(rows, grad_rows)
-    grad_copy = send(grad_out.at[0], grad_out.at[1], sg_.at[0], rg_.at[0], tok=peer)
-    grad_copy.start()
-    links.arrived(11)
+    links.start(far_square, square_in.at[2], square_in.at[3], shard=y)
+    back_last(1)
+    links.arrived(far_square)
     square_tok[0] = square_in[2] + square_in[3]
-    tok_copy = send(square_tok.at[0], square_tok.at[1], sn.at[0], rn.at[0], tok=peer)
-    tok_copy.start()
+    links.start(tok_square, square_tok.at[0], square_tok.at[1], tok=peer)
+    links.arrived(cen_link)
+    piece = cen_out.at[1, span(core, rows), :]
+    links.start(cen_twin, piece, piece, seg=twin)
 
     def own_back(first):
         r = tile_at(first)
         back_out[0, r, :] = back[r, span(tok, half_width)]
 
-    by_rows(rows, own_back)
-    tok_copy.wait()
+    by_rows(tokens, own_back)
+    links.arrived(tok_square)
     mse_out[...] = square_tok[0] + square_tok[1]
-    code_copy.wait()
-    cen_tok().wait_send()
-    cen_twin(1 - core).wait_recv()
-    cen_twin(core).wait_send()
-    for d in range(1, outer):
-        far_copy(d).wait_send()
-        far_twin(d, core).wait_send()
+    links.arrived(code_link, cen_twin)
+    for t in range(2):
+        for q in range(2):
+            back_tok(t, peer * 2 + q).wait()
+        links.arrived(t * stride + 11)
     links.finish()
-    for q in range(per_half):
-        back_tok(peer * per_half + q, q).wait()
-    grad_copy.wait()
 
 
 def vmem(count):
@@ -642,7 +689,7 @@
     n, outer = lax.axis_size("shard"), lax.axis_size("seg") // 2
     rows, depth = mlp.shape
     width, latents = depth // n, enc.shape[1]
-    part, far, half = rows // 2, max(outer - 1, 1), depth // 2
+    part, far, half = rows // 4, max(outer - 1, 1), depth // 2
     tokens = rows * lax.axis_size("tok")
     shape = jax.ShapeDtypeStruct
     return pl.pallas_call(
@@ -659,17 +706,17 @@
         scratch_shapes=[
             pltpu.VMEM((rows, depth), BF16),
             pltpu.VMEM((rows, latents), F32),
-            *scatter_bufs((), rows, width),
+            *scatter_bufs((2,), rows // 2, width),
             pltpu.VMEM((rows, width), F32),
             pltpu.VMEM((rows, width), F32),
-            pltpu.VMEM((far, part, width), BF16),
+            pltpu.VMEM((2, far, part, width), BF16),
             pltpu.VMEM((far, rows, width), BF16),
             pltpu.VMEM((rows, depth), BF16),
             pltpu.VMEM((rows, latents), F32),
             pltpu.VMEM((TILE, width), F32),
             pltpu.VMEM((n, 8, 128), F32),
             pltpu.VMEM((2, 8, 128), F32),
-            *sems(12, 1, 1, 1, 1, outer - 1, outer - 1, n // 2, 1, 1),
+            *sems(30 + 4 * (outer - 1), 4),
         ],
         compiler_params=params(1),
         name="sae",

time: 180 us -> 160 us (0.89)
  Pallas kernels: 167 us -> 147 us
    pallas_call x1, Pallas kernels: 91.1 us -> 71.3 us  [sae_call(): pl.pallas_call(functools.partial(sae_kernel, outer, 1.0 / math.sqrt(token...]
where the time goes in v3:
time: 160 us; the launch traced here: 159 us
  Pallas kernels  147 us (92%)
  matrix products  7.09 us (4%)
  local copies, waits for them, and re-layouts  2.26 us (1%)
  other arithmetic  1.94 us (1%)
    pallas_call x1, Pallas kernels, mlp_call(): pl.pallas_call(functools.partial(mlp_kernel, outer), out_shape=jax.ShapeD...  75.7 us
    pallas_call x1, Pallas kernels, sae_call(): pl.pallas_call(functools.partial(sae_kernel, outer, 1.0 / math.sqrt(token...  71.3 us
    dot_general x2, matrix products, over_tokens(): lax.dot_general(a, b, (((0,), (0,)), ((), ())), preferred_element_type=F32)  7.09 us

profile of v3, /device:TPU:10, one launch (start us, length us, event | category | flops | bytes accessed | tf_op | source)
XLA Modules:
  0.0 159.0 jit_solution(1493720128290468681)
XLA Ops:
  0.6 1.3 fusion
  1.9 0.7 compare_convert_fusion.live
  2.6 0.7 broadcast_in_dim.12.dec_bias
  3.3 0.0 copy-start
  3.3 1.0 copy-done
  4.3 0.0 copy-start.1
  4.3 75.7 %mlp.1 = bf16[384,2560]{1,0:T(8,128)(2,1)} custom-call(bf16[384,640]{1,0:T(8,128)(2,1)S(1)} %copy-done, bf16[640,2560]{1,0:T(8,128)(2,1)} %wg.1, bf16[640,2560]{1,0:T(8,128)(2,1)} %wu.1, bf16[2560,640]{1,0:T(8,128)(2,1)} %wd.1), custom_call_target="tpu_custom_call" | custom-call | tf_op jit(solution)/shard_map/mlp/pallas_call | solution.py:667
  80.1 0.0 copy-done.1
  80.1 71.3 %sae.1 = (bf16[2,384,1280]{2,1,0:T(8,128)(2,1)}, bf16[2,384,512]{2,1,0:T(8,128)(2,1)S(1)}, bf16[2,384,1280]{2,1,0:T(8,128)(2,1)}, bf16[2,384,512]{2,1,0:T(8,128)(2,1)S(1)}, f32[8,128]{1,0:T(8,128)S(1)}) custom-call(bf16[384,2560]{1,0:T(8,128)(2,1)} %mlp.1, bf16[2560,512]{1,0:T(8,128)(2,1)} %enc.1, f32[1,512]{1,0:T(1,128)S(1)} %bitcast.10, ...), custom_call_target="tpu_custom_call" | custom-call | tf_op jit(solution)/shard_map/sae/pallas_call | solution.py:695
  151.4 0.5 slice.3
  151.9 0.0 copy-start.2
  151.9 4.4 %convolution_bitcast_fusion.1 = f32[1280,512]{1,0:T(8,128)} fusion(bf16[2,384,1280]{2,1,0:T(8,128)(2,1)} %get-tuple-element.8, bf16[2,384,512]{2,1,0:T(8,128)(2,1)S(1)} %get-tuple-element.9), kind=kOutput, calls=%fused_computation.1 | convolution fusion | flops 1006632960 | bytes 5373952 | tf_op jit(solution)/shard_map/dot_general | solution.py:774
  156.3 0.0 copy-done.2
  156.3 2.7 %convolution_bitcast_fusion = f32[512,1280]{1,0:T(8,128)} fusion(bf16[2,384,512]{2,1,0:T(8,128)(2,1)S(1)} %get-tuple-element.10, bf16[2,384,1280]{2,1,0:T(8,128)(2,1)S(1)} %copy-done.2), kind=kOutput, calls=%fused_computation | convolution fusion | flops 1006632960 | bytes 5373952 | tf_op jit(solution)/shard_map/dot_general | solution.py:774
Async XLA Ops:
  3.3 1.0 copy-start
  4.3 75.7 %copy-start.1 = (f32[512]{0:T(512)S(1)}, f32[512]{0:T(512)}, u32[]{:S(2)}) copy-start(f32[512]{0:T(512)} %param.14) | copy-start | bytes 6148
  151.9 4.4 %copy-start.2 = (bf16[2,384,1280]{2,1,0:T(8,128)(2,1)S(1)}, bf16[2,384,1280]{2,1,0:T(8,128)(2,1)}, u32[]{:S(2)}) copy-start(bf16[2,384,1280]{2,1,0:T(8,128)(2,1)} %get-tuple-element.11) | copy-start | bytes 5898244

commit v4 on v3

--- a/solution.py
+++ b/solution.py
@@ -235,8 +235,8 @@
     links.start(base + 3, block(y, 1), block(y, 1), shard=x)
 
 
-def mlp_kernel(
-    outer, act, wg, wu, wd, out,
+def mlp_steps(
+    outer, down_ready, act, wg, wu, wd, out,
     to_corner, to_x, to_y, via_x, via_y, from_x, from_y,
     gate, up, hid, down, got, half, far, sent, arrived,
 ):
@@ -252,11 +252,6 @@
     small = part // 2
     links = Links(sent, arrived)
     stride = 19 + outer - 1
-    greet(
-        [{"shard": x}, {"shard": y}, {"seg": twin}]
-        + [{"seg": ((group + d) % outer) * 2 + core} for d in range(1, outer)]
-    )
-
     def bufs(t):
         return [b.at[t] for b in (to_corner, to_x, to_y, via_x, via_y, from_x, from_y)]
 
@@ -371,6 +366,7 @@
     partial_forward(1)
     partial_own(1)
     hidden_forward(0)
+    down_ready()
     down_near(0)
     hidden_start(1)
     down_start(0)
@@ -383,15 +379,19 @@
     out_forward(0)
     out_last(0)
     out_start(1)
+    links.arrived(*(15 + k for k in range(4)))
+    yield
     out_forward(1)
+    yield
     out_last(1)
-    for t in range(2):
-        links.arrived(*(t * stride + 15 + k for k in range(4)))
+    links.arrived(*(stride + 15 + k for k in range(4)))
+    yield
     links.finish()
-
-
-def sae_kernel(
-    outer, scale, count, mlp, enc, enc_bias, dec, dec_bias, live,
+    yield
+
+
+def sae_steps(
+    outer, scale, count, mlp, enc, enc_bias, dec, dec_bias, sizes,
     cen_out, code_out, back_out, grad_out, mse_out,
     cen, slope, to_corner, to_x, to_y, via_x, via_y, from_x, from_y, mine, other, payload, far,
     back, acc, squares, square_in, square_tok, sent, arrived, back_sent, back_arrived,
@@ -413,11 +413,6 @@
     code_link, cen_link, cen_twin, near_square, far_square, tok_square = (
         2 * stride + k for k in range(6)
     )
-    greet(
-        [{"shard": x}, {"shard": y}, {"seg": twin}, {"tok": peer}]
-        + [{"seg": ((group + d) % outer) * 2 + core} for d in range(1, outer)]
-    )
-
     def center_rows(first):
         r = tile_at(first)
         cen[r, :] = (mlp[r, :].astype(F32) - dec_bias[...]).astype(BF16)
@@ -436,7 +431,8 @@
         def columns(i, carry):
             c = span(i, step)
             pre = 10.0 * (dot(cen[half_of(t), :], enc[:, c]) + enc_bias[:, c])
-            on = live[:, c] > 0.0
+            index = me * latents + i * step + lax.broadcasted_iota(jnp.int32, (1, step), 1)
+            on = index < sizes[sg]
             soft = jnp.maximum(pre, 0.0) + jnp.log1p(jnp.exp(-jnp.abs(pre)))
             code_out[0, half_of(t), c] = jnp.where(on, soft / 10.0, 0.0).astype(BF16)
             slope[half_of(t), c] = jnp.where(on, jax.nn.sigmoid(pre), 0.0)
@@ -579,9 +575,12 @@
         )
 
     squares[...] = jnp.zeros_like(squares)
-    by_rows(tokens, center_rows)
+    by_rows(rows, center_rows)
     encode(0)
+    yield
     part_start(0)
+    yield
+    by_rows(rows, lambda first: center_rows(rows + first))
     links.start(
         cen_link,
         cen.at[span(core, rows), span(peer, half_width)],
@@ -635,6 +634,44 @@
             back_tok(t, peer * 2 + q).wait()
         links.arrived(t * stride + 11)
     links.finish()
+    yield
+
+
+def step_kernel(
+    outer, scale, count, mlp_count,
+    act, wg_far, wu_far, wd_far, enc_far, enc_bias, dec_far, dec_bias, sizes,
+    cen_out, code_out, back_out, grad_out, mse_out,
+    wg, wu, wd, enc, dec, mlp, load_sems, *scratch,
+):
+    pairs = ((wg_far, wg), (wu_far, wu), (wd_far, wd), (enc_far, enc), (dec_far, dec))
+    loads = [
+        pltpu.make_async_copy(src, dst, load_sems.at[k]) for k, (src, dst) in enumerate(pairs)
+    ]
+    for load in loads:
+        load.start()
+    me, sg, tok = lax.axis_index("shard"), lax.axis_index("seg"), lax.axis_index("tok")
+    core, group = sg % 2, sg // 2
+    x, y, _ = square_of(me)
+    greet(
+        [{"shard": x}, {"shard": y}, {"seg": sg + 1 - 2 * core}, {"tok": 1 - tok}]
+        + [{"seg": ((group + d) % outer) * 2 + core} for d in range(1, outer)]
+    )
+    loads[0].wait()
+    loads[1].wait()
+    first = mlp_steps(outer, loads[2].wait, act, wg, wu, wd, mlp, *scratch[:mlp_count])
+    second = sae_steps(
+        outer, scale, count, mlp, enc, enc_bias, dec, dec_bias, sizes,
+        cen_out, code_out, back_out, grad_out, mse_out, *scratch[mlp_count:],
+    )
+    next(first)
+    loads[3].wait()
+    loads[4].wait()
+    next(second)
+    next(first)
+    next(second)
+    next(first)
+    next(second)
+    next(first)
 
 
 def vmem(count):
@@ -659,68 +696,67 @@
     return [pltpu.VMEM(shape, BF16) for shape in (whole,) * 3 + (half,) * 2 + (whole,) * 2]
 
 
-def mlp_call(activations, gate_weight, up_weight, down_weight):
+def step_call(act, wg, wu, wd, enc, enc_bias, dec, dec_bias, sizes):
     n, outer = lax.axis_size("shard"), lax.axis_size("seg") // 2
-    tokens = activations.shape[0]
-    chunk, width = gate_weight.shape[1] // n, down_weight.shape[1]
-    rows, part, far = tokens // 2, tokens // 4, max(outer - 1, 1)
+    tokens, far = act.shape[0], max(outer - 1, 1)
+    rows, part = tokens // 2, tokens // 4
+    chunk, width = wg.shape[1] // n, wd.shape[1]
+    depth, latents, half = width * n, enc.shape[1], width * n // 2
+    total = tokens * lax.axis_size("tok")
+    shape = jax.ShapeDtypeStruct
+    mlp_scratch = [
+        *scatter_bufs((2,), rows, 2 * chunk),
+        pltpu.VMEM((2, rows, chunk), F32),
+        pltpu.VMEM((2, rows, chunk), F32),
+        pltpu.VMEM((2, n, rows, chunk), BF16),
+        pltpu.VMEM((2, rows, width), F32),
+        pltpu.VMEM((2, part, width), F32),
+        pltpu.VMEM((2, part, width), BF16),
+        pltpu.VMEM((2, far, part, width), BF16),
+        *sems(2 * (18 + outer)),
+    ]
+    sae_scratch = [
+        pltpu.VMEM((tokens, depth), BF16),
+        pltpu.VMEM((tokens, latents), F32),
+        *scatter_bufs((2,), rows, width),
+        pltpu.VMEM((tokens, width), F32),
+        pltpu.VMEM((tokens, width), F32),
+        pltpu.VMEM((2, far, part, width), BF16),
+        pltpu.VMEM((far, tokens, width), BF16),
+        pltpu.VMEM((tokens, depth), BF16),
+        pltpu.VMEM((tokens, latents), F32),
+        pltpu.VMEM((TILE, width), F32),
+        pltpu.VMEM((n, 8, 128), F32),
+        pltpu.VMEM((2, 8, 128), F32),
+        *sems(30 + 4 * (outer - 1), 4),
+    ]
+    inside, outside = pl.BlockSpec(memory_space=pltpu.VMEM), pl.BlockSpec(memory_space=pl.ANY)
     return pl.pallas_call(
-        functools.partial(mlp_kernel, outer),
-        out_shape=jax.ShapeDtypeStruct((tokens, width * n), BF16),
-        in_specs=vmem(4),
-        out_specs=vmem(1)[0],
+        functools.partial(
+            step_kernel, outer, 1.0 / math.sqrt(total), total * depth, len(mlp_scratch)
+        ),
+        out_shape=(
+            shape((2, tokens, half), BF16),
+            shape((2, tokens, latents), BF16),
+            shape((2, tokens, half), BF16),
+            shape((2, tokens, latents), BF16),
+            shape((8, 128), F32),
+        ),
+        in_specs=[
+            inside, outside, outside, outside, outside, inside, outside, inside,
+            pl.BlockSpec(memory_space=pltpu.SMEM),
+        ],
+        out_specs=tuple(vmem(5)),
         scratch_shapes=[
-            *scatter_bufs((2,), rows, 2 * chunk),
-            pltpu.VMEM((2, rows, chunk), F32),
-            pltpu.VMEM((2, rows, chunk), F32),
-            pltpu.VMEM((2, n, rows, chunk), BF16),
-            pltpu.VMEM((2, rows, width), F32),
-            pltpu.VMEM((2, part, width), F32),
-            pltpu.VMEM((2, part, width), BF16),
-            pltpu.VMEM((2, far, part, width), BF16),
-            *sems(2 * (18 + outer)),
+            *(pltpu.VMEM(value.shape, BF16) for value in (wg, wu, wd, enc, dec)),
+            pltpu.VMEM((tokens, depth), BF16),
+            pltpu.SemaphoreType.DMA((5,)),
+            *mlp_scratch,
+            *sae_scratch,
         ],
         compiler_params=params(0),
-        name="mlp",
-    )(activations, gate_weight, up_weight, down_weight)
-
-
-def sae_call(mlp, enc, enc_bias, dec, dec_bias, live):
-    n, outer = lax.axis_size("shard"), lax.axis_size("seg") // 2
-    rows, depth = mlp.shape
-    width, latents = depth // n, enc.shape[1]
-    part, far, half = rows // 4, max(outer - 1, 1), depth // 2
-    tokens = rows * lax.axis_size("tok")
-    shape = jax.ShapeDtypeStruct
-    return pl.pallas_call(
-        functools.partial(sae_kernel, outer, 1.0 / math.sqrt(tokens), tokens * depth),
-        out_shape=(
-            shape((2, rows, half), BF16),
-            shape((2, rows, latents), BF16),
-            shape((2, rows, half), BF16),
-            shape((2, rows, latents), BF16),
-            shape((8, 128), F32),
-        ),
-        in_specs=vmem(6),
-        out_specs=tuple(vmem(5)),
-        scratch_shapes=[
-            pltpu.VMEM((rows, depth), BF16),
-            pltpu.VMEM((rows, latents), F32),
-            *scatter_bufs((2,), rows // 2, width),
-            pltpu.VMEM((rows, width), F32),
-            pltpu.VMEM((rows, width), F32),
-            pltpu.VMEM((2, far, part, width), BF16),
-            pltpu.VMEM((far, rows, width), BF16),
-            pltpu.VMEM((rows, depth), BF16),
-            pltpu.VMEM((rows, latents), F32),
-            pltpu.VMEM((TILE, width), F32),
-            pltpu.VMEM((n, 8, 128), F32),
-            pltpu.VMEM((2, 8, 128), F32),
-            *sems(30 + 4 * (outer - 1), 4),
-        ],
-        compiler_params=params(1),
-        name="sae",
-    )(mlp, enc, enc_bias, dec, dec_bias, live)
+        name="step",
+    )(act, wg, wu, wd, enc, enc_bias, dec, dec_bias, sizes)
 
 
 def fits(activations, gate_weight, encoder_weight):
@@ -759,14 +795,16 @@
             decoder_bias,
             segment_sizes,
         )
-    latents = encoder_weight.shape[1]
-    here = jnp.arange(segment_sizes.shape[0]) == lax.axis_index("seg")
-    size_here = jnp.sum(jnp.where(here, segment_sizes, 0))
-    index = lax.axis_index("shard") * latents + jnp.arange(latents)
-    live = (index < size_here).astype(F32)[None, :]
-    mlp = mlp_call(activations, gate_weight, up_weight, down_weight)
-    cen, codes, back, code_grad, mse = sae_call(
-        mlp, encoder_weight, encoder_bias[None, :], decoder_weight, decoder_bias[None, :], live
+    cen, codes, back, code_grad, mse = step_call(
+        activations,
+        gate_weight,
+        up_weight,
+        down_weight,
+        encoder_weight,
+        encoder_bias[None, :],
+        decoder_weight,
+        decoder_bias[None, :],
+        segment_sizes,
     )
 
     def over_tokens(a, b):

time: 160 us -> 147 us (0.919)
  Pallas kernels: 147 us -> 133 us
  other arithmetic: 1.94 us -> 0 us
    pallas_call x2 -> x1, Pallas kernels: 147 us -> 133 us  [step_call(): pl.pallas_call(functools.partial(step_kernel, outer, 1.0 / math.sqrt(tota...]
where the time goes in v4:
time: 147 us; the launch traced here: 145 us
  Pallas kernels  133 us (90%)
  matrix products  7.27 us (5%)
  local copies, waits for them, and re-layouts  3.59 us (2%)
    pallas_call x1, Pallas kernels, step_call(): pl.pallas_call(functools.partial(step_kernel, outer, 1.0 / math.sqrt(tota...  133 us
    dot_general x2, matrix products, over_tokens(): lax.dot_general(a, b, (((0,), (0,)), ((), ())), preferred_element_type=F32)  7.27 us

profile of v4, /device:TPU:10, one launch (start us, length us, event | category | flops | bytes accessed | tf_op | source)
XLA Modules:
  0.0 144.6 jit_solution(344725719774792908)
XLA Ops:
  0.6 0.7 broadcast_in_dim.7.dec_bias
  1.3 0.0 copy-start
  1.4 1.0 copy-done
  2.4 0.0 copy-start.1
  2.4 0.7 copy-done.1
  3.1 0.0 copy-start.2
  3.1 0.7 copy-done.2
  3.7 133.1 %step.1 = (bf16[2,384,1280]{2,1,0:T(8,128)(2,1)}, bf16[2,384,512]{2,1,0:T(8,128)(2,1)S(1)}, bf16[2,384,1280]{2,1,0:T(8,128)(2,1)}, bf16[2,384,512]{2,1,0:T(8,128)(2,1)}, f32[8,128]{1,0:T(8,128)S(1)}) custom-call(bf16[384,640]{1,0:T(8,128)(2,1)S(1)} %copy-done, bf16[640,2560]{1,0:T(8,128)(2,1)} %wg_far.1, bf16[640,2560]{1,0:T(8,128)(2,1)} %wu_far.1, ...), custom_call_target="tpu_custom_call" | custom-call | tf_op jit(solution)/shard_map/step/pallas_call | solution.py:734
  136.9 0.5 slice.3
  137.4 0.0 copy-start.3
  137.4 4.6 %convolution_bitcast_fusion.1 = f32[1280,512]{1,0:T(8,128)} fusion(bf16[2,384,1280]{2,1,0:T(8,128)(2,1)} %get-tuple-element.8, bf16[2,384,512]{2,1,0:T(8,128)(2,1)} %get-tuple-element.9), kind=kOutput, calls=%fused_computation.1 | convolution fusion | flops 1006632960 | bytes 5373952 | tf_op jit(solution)/shard_map/dot_general | solution.py:812
  141.9 0.0 copy-done.3
  141.9 2.7 %convolution_bitcast_fusion = f32[512,1280]{1,0:T(8,128)} fusion(bf16[2,384,512]{2,1,0:T(8,128)(2,1)S(1)} %get-tuple-element.10, bf16[2,384,1280]{2,1,0:T(8,128)(2,1)S(1)} %copy-done.3), kind=kOutput, calls=%fused_computation | convolution fusion | flops 1006632960 | bytes 5373952 | tf_op jit(solution)/shard_map/dot_general | solution.py:812
Async XLA Ops:
  1.3 1.0 copy-start
  2.4 0.7 copy-start.1
  3.1 0.7 copy-start.2
  137.4 4.6 %copy-start.3 = (bf16[2,384,1280]{2,1,0:T(8,128)(2,1)S(1)}, bf16[2,384,1280]{2,1,0:T(8,128)(2,1)}, u32[]{:S(2)}) copy-start(bf16[2,384,1280]{2,1,0:T(8,128)(2,1)} %get-tuple-element.11) | copy-start | bytes 5898244

commit v5 on v4

--- a/solution.py
+++ b/solution.py
@@ -410,9 +410,8 @@
     rows = tokens // 2
     part = rows // 2
     stride = 12 + 2 * (outer - 1)
-    code_link, cen_link, cen_twin, near_square, far_square, tok_square = (
-        2 * stride + k for k in range(6)
-    )
+    near_square, far_square, tok_square = (2 * stride + k for k in range(3))
+    code_link, cen_link, cen_twin = (2 * stride + 3 + 2 * k for k in range(3))
     def center_rows(first):
         r = tile_at(first)
         cen[r, :] = (mlp[r, :].astype(F32) - dec_bias[...]).astype(BF16)
@@ -494,6 +493,27 @@
             links.arrived(t * stride + 11 + d)
             piece = far.at[d - 1, core_rows(t), :]
             links.start(t * stride + 10 + outer + d, piece, piece, seg=twin)
+
+    def cen_start(t):
+        links.start(
+            cen_link + t,
+            cen.at[core_rows(t), span(peer, half_width)],
+            cen_out.at[1, core_rows(t), :],
+            tok=peer,
+        )
+
+    def cen_pass(t):
+        links.arrived(cen_link + t)
+        piece = cen_out.at[1, core_rows(t), :]
+        links.start(cen_twin + t, piece, piece, seg=twin)
+
+    def code_start(t):
+        links.start(
+            code_link + t,
+            code_out.at[0, half_of(t), :],
+            code_out.at[1, half_of(t), :],
+            tok=peer,
+        )
 
     ahead = (segments - sg).astype(F32)
     other_error = core.astype(F32)
@@ -576,17 +596,14 @@
 
     squares[...] = jnp.zeros_like(squares)
     by_rows(rows, center_rows)
+    cen_start(0)
     encode(0)
+    code_start(0)
     yield
     part_start(0)
     yield
     by_rows(rows, lambda first: center_rows(rows + first))
-    links.start(
-        cen_link,
-        cen.at[span(core, rows), span(peer, half_width)],
-        cen_out.at[1, span(core, rows), :],
-        tok=peer,
-    )
+    cen_start(1)
     encode(1)
     part_forward(0)
     part_start(1)
@@ -595,7 +612,7 @@
     part_forward(1)
     far_start(0)
     part_own(1)
-    links.start(code_link, code_out.at[0], code_out.at[1], tok=peer)
+    code_start(1)
     far_pass(0)
     part_sum(1)
     back_start(0)
@@ -617,9 +634,8 @@
     links.arrived(far_square)
     square_tok[0] = square_in[2] + square_in[3]
     links.start(tok_square, square_tok.at[0], square_tok.at[1], tok=peer)
-    links.arrived(cen_link)
-    piece = cen_out.at[1, span(core, rows), :]
-    links.start(cen_twin, piece, piece, seg=twin)
+    for t in range(2):
+        cen_pass(t)
 
     def own_back(first):
         r = tile_at(first)
@@ -628,8 +644,8 @@
     by_rows(tokens, own_back)
     links.arrived(tok_square)
     mse_out[...] = square_tok[0] + square_tok[1]
-    links.arrived(code_link, cen_twin)
     for t in range(2):
+        links.arrived(code_link + t, cen_twin + t)
         for q in range(2):
             back_tok(t, peer * 2 + q).wait()
         links.arrived(t * stride + 11)
@@ -728,7 +744,7 @@
         pltpu.VMEM((TILE, width), F32),
         pltpu.VMEM((n, 8, 128), F32),
         pltpu.VMEM((2, 8, 128), F32),
-        *sems(30 + 4 * (outer - 1), 4),
+        *sems(33 + 4 * (outer - 1), 4),
     ]
     inside, outside = pl.BlockSpec(memory_space=pltpu.VMEM), pl.BlockSpec(memory_space=pl.ANY)
     return pl.pallas_call(

time: 147 us -> 145 us (0.986)
  Pallas kernels: 133 us -> 131 us
    pallas_call x1, Pallas kernels: 133 us -> 131 us  [step_call(): pl.pallas_call(functools.partial(step_kernel, outer, 1.0 / math.sqrt(tota...]
where the time goes in v5:
time: 145 us; the launch traced here: 142 us
  Pallas kernels  131 us (90%)
  matrix products  7.27 us (5%)
  local copies, waits for them, and re-layouts  3.59 us (2%)
    pallas_call x1, Pallas kernels, step_call(): pl.pallas_call(functools.partial(step_kernel, outer, 1.0 / math.sqrt(tota...  131 us
    dot_general x2, matrix products, over_tokens(): lax.dot_general(a, b, (((0,), (0,)), ((), ())), preferred_element_type=F32)  7.27 us

profile of v5, /device:TPU:10, one launch (start us, length us, event | category | flops | bytes accessed | tf_op | source)
XLA Modules:
  0.0 142.3 jit_solution(2500781440582496918)
XLA Ops:
  0.6 0.7 broadcast_in_dim.7.dec_bias
  1.3 0.0 copy-start
  1.4 1.0 copy-done
  2.4 0.0 copy-start.1
  2.4 0.7 copy-done.1
  3.1 0.0 copy-start.2
  3.1 0.7 copy-done.2
  3.7 130.8 %step.1 = (bf16[2,384,1280]{2,1,0:T(8,128)(2,1)}, bf16[2,384,512]{2,1,0:T(8,128)(2,1)S(1)}, bf16[2,384,1280]{2,1,0:T(8,128)(2,1)}, bf16[2,384,512]{2,1,0:T(8,128)(2,1)}, f32[8,128]{1,0:T(8,128)S(1)}) custom-call(bf16[384,640]{1,0:T(8,128)(2,1)S(1)} %copy-done, bf16[640,2560]{1,0:T(8,128)(2,1)} %wg_far.1, bf16[640,2560]{1,0:T(8,128)(2,1)} %wu_far.1, ...), custom_call_target="tpu_custom_call" | custom-call | tf_op jit(solution)/shard_map/step/pallas_call | solution.py:750
  134.5 0.5 slice.3
  135.1 0.0 copy-start.3
  135.1 4.6 %convolution_bitcast_fusion.1 = f32[1280,512]{1,0:T(8,128)} fusion(bf16[2,384,1280]{2,1,0:T(8,128)(2,1)} %get-tuple-element.8, bf16[2,384,512]{2,1,0:T(8,128)(2,1)} %get-tuple-element.9), kind=kOutput, calls=%fused_computation.1 | convolution fusion | flops 1006632960 | bytes 5373952 | tf_op jit(solution)/shard_map/dot_general | solution.py:828
  139.6 0.0 copy-done.3
  139.6 2.7 %convolution_bitcast_fusion = f32[512,1280]{1,0:T(8,128)} fusion(bf16[2,384,512]{2,1,0:T(8,128)(2,1)S(1)} %get-tuple-element.10, bf16[2,384,1280]{2,1,0:T(8,128)(2,1)S(1)} %copy-done.3), kind=kOutput, calls=%fused_computation | convolution fusion | flops 1006632960 | bytes 5373952 | tf_op jit(solution)/shard_map/dot_general | solution.py:828
Async XLA Ops:
  1.3 1.0 copy-start
  2.4 0.7 copy-start.1
  3.1 0.7 copy-start.2
  135.1 4.6 %copy-start.3 = (bf16[2,384,1280]{2,1,0:T(8,128)(2,1)S(1)}, bf16[2,384,1280]{2,1,0:T(8,128)(2,1)}, u32[]{:S(2)}) copy-start(bf16[2,384,1280]{2,1,0:T(8,128)(2,1)} %get-tuple-element.11) | copy-start | bytes 5898244
